TPU v7x, 32 devices: a whole 2x2x4 slice. The times are simulated.
32 devices in a mesh: dp: 8 (over z, y), expert: 4 (over x, core).
Axes of the slice: x: 2, y: 2, z: 4, core: 2. Of those that a mesh axis runs over, the one named last changes fastest.
Arguments:
- hidden_in: bfloat16 [32768, 768], P(('dp', 'expert')), may hold values from -6 to 6
- gate_prior: float32 [32768, 8], P(('dp', 'expert')), may hold values from -6 to 6
- routes: int32 [32768, 2], P(('dp', 'expert')), may hold values from 0 to 7, all different within a row
- priority: int32 [32, 1024], P(('dp', 'expert')), may hold values from 0 to 1023, each once within a row
- segments: int32 [32, 1024], P(('dp', 'expert')), may hold values from 0 to 5, never falling along the last dimension, each value on 1 to 768 neighbouring positions
- cotangent: bfloat16 [32768, 768], P(('dp', 'expert')), may hold values from -6 to 6
- attend_in: float32 [768, 2304], P(('dp', 'expert')), may hold values from -0.21875 to 0.21875
- first_attend_in: float32 [768, 2304], P(('dp', 'expert')), may hold values from -0.0029296875 to 0.0029296875
- second_attend_in: float32 [768, 2304], P(('dp', 'expert')), may hold values from 1e-08 to 1e-07
- attend_out: float32 [768, 768], P(('dp', 'expert')), may hold values from -1.25 to 1.25
- first_attend_out: float32 [768, 768], P(('dp', 'expert')), may hold values from -0.0029296875 to 0.0029296875
- second_attend_out: float32 [768, 768], P(('dp', 'expert')), may hold values from 1e-08 to 1e-07
- router: float32 [768, 8], P(('dp', 'expert')), may hold values from -0.109375 to 0.109375
- first_router: float32 [768, 8], P(('dp', 'expert')), may hold values from -0.0029296875 to 0.0029296875
- second_router: float32 [768, 8], P(('dp', 'expert')), may hold values from 1e-08 to 1e-07
- gate_mix: float32 [8, 8], replicated, may hold values from -1 to 1
- first_gate_mix: float32 [8, 8], replicated, may hold values from -0.0029296875 to 0.0029296875
- second_gate_mix: float32 [8, 8], replicated, may hold values from 1e-08 to 1e-07
- constants: float32 [768, 6], P(('dp', 'expert')), may hold values from -0.4375 to 0.4375
- first_constants: float32 [768, 6], P(('dp', 'expert')), may hold values from -0.0029296875 to 0.0029296875
- second_constants: float32 [768, 6], P(('dp', 'expert')), may hold values from 1e-08 to 1e-07
- norm_gains: float32 [2, 768], P(None, ('dp', 'expert')), may hold values from 0.5 to 1.5
- first_norm_gains: float32 [2, 768], P(None, ('dp', 'expert')), may hold values from -0.0029296875 to 0.0029296875
- second_norm_gains: float32 [2, 768], P(None, ('dp', 'expert')), may hold values from 1e-08 to 1e-05
- expert_in: float32 [4, 768, 4096], P('expert', 'dp'), may hold values from -0.21875 to 0.21875
- first_expert_in: float32 [4, 768, 4096], P('expert', 'dp'), may hold values from -0.0029296875 to 0.0029296875
- second_expert_in: float32 [4, 768, 4096], P('expert', 'dp'), may hold values from 1e-08 to 1e-07
- expert_out: float32 [4, 2048, 768], P('expert', 'dp'), may hold values from -0.5 to 0.5
- first_expert_out: float32 [4, 2048, 768], P('expert', 'dp'), may hold values from -0.0029296875 to 0.0029296875
- second_expert_out: float32 [4, 2048, 768], P('expert', 'dp'), may hold values from 1e-11 to 1e-08
Outputs:
- activations: bfloat16 [32768, 768], P(('dp', 'expert'))
- input_grad: float32 [32768, 768], P(('dp', 'expert'))
- grad_norm: float32 [], replicated
- grad_attend_in: float32 [768, 2304], P(('dp', 'expert'))
- new_attend_in: float32 [768, 2304], P(('dp', 'expert'))
- new_first_attend_in: float32 [768, 2304], P(('dp', 'expert'))
- new_second_attend_in: float32 [768, 2304], P(('dp', 'expert'))
- copy_attend_in: bfloat16 [768, 2304], P(('dp', 'expert'))
- grad_attend_out: float32 [768, 768], P(('dp', 'expert'))
- new_attend_out: float32 [768, 768], P(('dp', 'expert'))
- new_first_attend_out: float32 [768, 768], P(('dp', 'expert'))
- new_second_attend_out: float32 [768, 768], P(('dp', 'expert'))
- copy_attend_out: bfloat16 [768, 768], P(('dp', 'expert'))
- grad_router: float32 [768, 8], P(('dp', 'expert'))
- new_router: float32 [768, 8], P(('dp', 'expert'))
- new_first_router: float32 [768, 8], P(('dp', 'expert'))
- new_second_router: float32 [768, 8], P(('dp', 'expert'))
- copy_router: bfloat16 [768, 8], P(('dp', 'expert'))
- grad_gate_mix: float32 [8, 8], replicated
- new_gate_mix: float32 [8, 8], replicated
- new_first_gate_mix: float32 [8, 8], replicated
- new_second_gate_mix: float32 [8, 8], replicated
- copy_gate_mix: bfloat16 [8, 8], replicated
- grad_constants: float32 [768, 6], P(('dp', 'expert'))
- new_constants: float32 [768, 6], P(('dp', 'expert'))
- new_first_constants: float32 [768, 6], P(('dp', 'expert'))
- new_second_constants: float32 [768, 6], P(('dp', 'expert'))
- copy_constants: bfloat16 [768, 6], P(('dp', 'expert'))
- grad_norm_gains: float32 [2, 768], P(None, ('dp', 'expert'))
- new_norm_gains: float32 [2, 768], P(None, ('dp', 'expert'))
- new_first_norm_gains: float32 [2, 768], P(None, ('dp', 'expert'))
- new_second_norm_gains: float32 [2, 768], P(None, ('dp', 'expert'))
- copy_norm_gains: bfloat16 [2, 768], P(None, ('dp', 'expert'))
- grad_expert_in: float32 [4, 768, 4096], P('expert', 'dp')
- new_expert_in: float32 [4, 768, 4096], P('expert', 'dp')
- new_first_expert_in: float32 [4, 768, 4096], P('expert', 'dp')
- new_second_expert_in: float32 [4, 768, 4096], P('expert', 'dp')
- copy_expert_in: bfloat16 [4, 768, 4096], P('expert', 'dp')
- grad_expert_out: float32 [4, 2048, 768], P('expert', 'dp')
- new_expert_out: float32 [4, 2048, 768], P('expert', 'dp')
- new_first_expert_out: float32 [4, 2048, 768], P('expert', 'dp')
- new_second_expert_out: float32 [4, 2048, 768], P('expert', 'dp')
- copy_expert_out: bfloat16 [4, 2048, 768], P('expert', 'dp')
Inputs may be any that keep to these rules, and one draw needn't show every extreme that they name: `routes`: each row names 2 different kinds; kinds below 4 are feed-forward experts, 4 the zero expert, 5 the copy expert, the rest constant experts. `priority`: each row is a permutation. `segments`: numbers never fall along a sequence; a document has 1 to 768 tokens.
All inputs are finite; a program needn't handle non-finite values.
Results may differ from a plain program's by a relative error of at most 0.013.
The roundings to bfloat16 on the way count: a program that leaves them out, or rounds other values in their place, can miss the bound.
Values may be sent and summed in bfloat16 or wider, within the bound.
No kernel may reach another device: no remote copies, remote signals or barrier semaphores. Data moves between devices by JAX's collectives and lax.ppermute only.
A program may use at most 320 MiB of HBM per device.

v0:
```python
import jax
import jax.numpy as jnp
from jax import lax
from jax.sharding import PartitionSpec as P

D = 768
FF = 2048
HEADS = 12
HEAD_DIM = 64
SEQ = 1024
SEQS_DEV = 1


norm_epsilon = 1e-05
adam_epsilon = 1e-08
learn_rates = (0.01, 0.04, 0.01, 0.03, 0.01, 0.1, 0.01, 0.01)
decay_rate = 0.1
beta_moment = 0.5
step_number = 4.0
clip_limit = 1.0
score_scale = 0.125
masked_score = -1e30
highest = lax.Precision.HIGHEST


def norm_rows(values, gain_row):
    scaling = lax.rsqrt(jnp.mean(values * values, axis=-1, keepdims=True) + norm_epsilon)
    return values * scaling * gain_row


def pair_tables(routes, priority, experts, total_kinds, capacity):
    tokens_here = routes.shape[0]
    width_top = routes.shape[1]
    kind_ids = jnp.arange(total_kinds, dtype=jnp.int32)
    one_hot = jnp.sum((routes[:, :, None] == kind_ids[None, None, :]).astype(jnp.float32), axis=1)
    earlier = (priority[None, :] < priority[:, None]).astype(jnp.float32)
    before = jnp.dot(earlier, one_hot, precision=highest)
    slots = jnp.take_along_axis(before, routes, axis=1).astype(jnp.int32)
    kept_pairs = jnp.logical_and(routes < experts, slots < capacity)
    targets = jnp.where(kept_pairs, routes * capacity + slots, experts * capacity)
    pair_ids = jnp.arange(tokens_here * width_top, dtype=jnp.int32)
    owners = jnp.full((experts * capacity,), tokens_here * width_top, dtype=jnp.int32)
    owners = owners.at[targets.reshape(-1)].set(pair_ids, mode="drop")
    return (targets, owners)


def mixture(normed, paired, router_w, mixer_w, constant_w, prior, routes, experts):
    logits = jnp.dot(normed, router_w, precision=highest) + jnp.dot(
        prior, mixer_w, precision=highest
    )
    probabilities = jax.nn.softmax(logits, axis=-1)
    chosen = jnp.take_along_axis(probabilities, routes, axis=1)
    constant_count = constant_w.shape[1] // 3
    gate_logits = jnp.dot(normed, constant_w[:, : 2 * constant_count], precision=highest)
    shares = jax.nn.softmax(gate_logits.reshape(normed.shape[0], constant_count, 2), axis=-1)
    blended = jnp.zeros_like(normed)
    for route_index in range(routes.shape[1]):
        expert_ids = routes[:, route_index : route_index + 1]
        branch_out = paired[:, route_index] + jnp.where(expert_ids == experts + 1, normed, 0.0)
        for const_index in range(constant_count):
            constant_term = (
                shares[:, const_index, 0:1] * normed
                + shares[:, const_index, 1:2]
                * constant_w[:, 2 * constant_count + const_index][None, :]
            )
            branch_out = branch_out + jnp.where(
                expert_ids == experts + 2 + const_index, constant_term, 0.0
            )
        blended = blended + chosen[:, route_index : route_index + 1] * branch_out
    return blended


def scores_of(queries, key_rows, segment):
    raw = jnp.einsum("qhd,khd->hqk", queries, key_rows, preferred_element_type=jnp.float32)
    places = jnp.arange(segment.shape[0], dtype=jnp.int32)
    allowed = jnp.logical_and(
        segment[:, None] == segment[None, :], places[None, :] <= places[:, None]
    )
    return jnp.where(allowed[None], raw * score_scale, masked_score)


def attend_forward(element):
    queries, key_rows, value_rows, segment = element
    scores = scores_of(queries, key_rows, segment)
    maximum = jnp.max(scores, axis=-1, keepdims=True)
    totals = jnp.sum(jnp.exp(scores - maximum), axis=-1, keepdims=True)
    logsum = maximum + jnp.log(totals)
    weights = jnp.exp(scores - logsum).astype(jnp.bfloat16)
    attended = jnp.einsum("hqk,khd->qhd", weights, value_rows, preferred_element_type=jnp.float32)
    return (attended.astype(jnp.bfloat16), logsum)


def attend_backward(element):
    queries, key_rows, value_rows, segment, logsum, grad_attended = element
    scores = scores_of(queries, key_rows, segment)
    weights = jnp.exp(scores - logsum)
    grad_weights = jnp.einsum(
        "qhd,khd->hqk", grad_attended, value_rows, preferred_element_type=jnp.float32
    )
    grad_values = jnp.einsum(
        "hqk,qhd->khd",
        weights.astype(jnp.bfloat16),
        grad_attended,
        preferred_element_type=jnp.float32,
    )
    centred = jnp.sum(weights * grad_weights, axis=-1, keepdims=True)
    grad_raw = (weights * (grad_weights - centred) * score_scale).astype(jnp.bfloat16)
    grad_queries = jnp.einsum(
        "hqk,khd->qhd", grad_raw, key_rows, preferred_element_type=jnp.float32
    )
    grad_keys = jnp.einsum("hqk,qhd->khd", grad_raw, queries, preferred_element_type=jnp.float32)
    return jnp.stack([grad_queries, grad_keys, grad_values], axis=1)


def adam_step(master, first, second, grad, factor, step_rate):
    clipped = grad * factor
    first_new = beta_moment * first + (1.0 - beta_moment) * clipped
    second_new = beta_moment * second + (1.0 - beta_moment) * clipped * clipped
    correct = 1.0 - beta_moment**step_number
    update = (
        first_new / correct / (jnp.sqrt(second_new / correct) + adam_epsilon) + decay_rate * master
    )
    master_new = master - step_rate * update
    return (grad, master_new, first_new, second_new, master_new.astype(jnp.bfloat16))


def body(
    hidden_in,
    gate_prior,
    routes,
    priority,
    segments,
    cotangent,
    attend_in,
    first_attend_in,
    second_attend_in,
    attend_out,
    first_attend_out,
    second_attend_out,
    router,
    first_router,
    second_router,
    gate_mix,
    first_gate_mix,
    second_gate_mix,
    constants,
    first_constants,
    second_constants,
    norm_gains,
    first_norm_gains,
    second_norm_gains,
    expert_in,
    first_expert_in,
    second_expert_in,
    expert_out,
    first_expert_out,
    second_expert_out,
):
    groups = lax.axis_size("expert")
    total_kinds = gate_prior.shape[1]
    constant_count = constants.shape[1] // 3
    experts = total_kinds - 2 - constant_count
    local_experts = expert_in.shape[0]
    token_count = hidden_in.shape[0]
    width_top = routes.shape[1]
    capacity = max(2, width_top * token_count // total_kinds // 8 * 8)
    weight_in, weight_out, router_full, constant_full, gains_full = (
        lax.all_gather(attend_in.astype(jnp.bfloat16), ("dp", "expert"), axis=0, tiled=True),
        lax.all_gather(attend_out.astype(jnp.bfloat16), ("dp", "expert"), axis=0, tiled=True),
        lax.all_gather(router.astype(jnp.bfloat16), ("dp", "expert"), axis=0, tiled=True),
        lax.all_gather(constants.astype(jnp.bfloat16), ("dp", "expert"), axis=0, tiled=True),
        lax.all_gather(norm_gains.astype(jnp.bfloat16), ("dp", "expert"), axis=1, tiled=True),
    )
    expert_inner, expert_outer = (
        lax.all_gather(expert_in.astype(jnp.bfloat16), "dp", axis=1, tiled=True),
        lax.all_gather(expert_out.astype(jnp.bfloat16), "dp", axis=1, tiled=True),
    )
    mixer = gate_mix.astype(jnp.bfloat16).astype(jnp.float32)
    gain_first = gains_full[0].astype(jnp.float32)
    gain_second = gains_full[1].astype(jnp.float32)
    hidden = hidden_in.astype(jnp.float32)
    normed_float, pull_first = jax.vjp(norm_rows, hidden, gain_first)
    normed_first = normed_float.astype(jnp.bfloat16)
    packed = jnp.dot(normed_first, weight_in, preferred_element_type=jnp.float32).astype(
        jnp.bfloat16
    )
    shaped = packed.reshape(SEQS_DEV, SEQ, 3, HEADS, HEAD_DIM)
    queries = shaped[:, :, 0]
    key_rows = shaped[:, :, 1]
    value_rows = shaped[:, :, 2]
    attended, logsums = lax.map(attend_forward, (queries, key_rows, value_rows, segments))
    attended_flat = attended.reshape(token_count, D)
    middle = hidden + jnp.dot(attended_flat, weight_out, preferred_element_type=jnp.float32)
    second_float, pull_second = jax.vjp(norm_rows, middle, gain_second)
    normed_second = second_float.astype(jnp.bfloat16)
    normed_values = normed_second.astype(jnp.float32)
    targets, owners = pair_tables(routes, priority[0], experts, total_kinds, capacity)
    outgoing = jnp.take(normed_second, owners // width_top, axis=0, mode="fill", fill_value=0)
    arrived = lax.all_to_all(
        outgoing.reshape(groups, local_experts * capacity, D),
        "expert",
        split_axis=0,
        concat_axis=0,
        tiled=True,
    )
    slot_rows = arrived.reshape(groups, local_experts, capacity, D)
    joined = jnp.einsum(
        "secd,edf->secf", slot_rows, expert_inner, preferred_element_type=jnp.float32
    )
    gate_part = joined[..., :FF]
    up_part = joined[..., FF:]
    activated = (jax.nn.silu(gate_part) * up_part).astype(jnp.bfloat16)
    produced = jnp.einsum(
        "secf,efd->secd", activated, expert_outer, preferred_element_type=jnp.float32
    ).astype(jnp.bfloat16)
    returned = lax.all_to_all(
        produced.reshape(groups, local_experts * capacity, D),
        "expert",
        split_axis=0,
        concat_axis=0,
        tiled=True,
    )
    pair_out = jnp.take(
        returned.reshape(experts * capacity, D), targets, axis=0, mode="fill", fill_value=0
    ).astype(jnp.float32)

    def mixing(normed, paired, router_w, mixer_w, constant_w):
        return mixture(normed, paired, router_w, mixer_w, constant_w, gate_prior, routes, experts)

    blended, pull_mix = jax.vjp(
        mixing,
        normed_values,
        pair_out,
        router_full.astype(jnp.float32),
        mixer,
        constant_full.astype(jnp.float32),
    )
    activations = (middle + blended).astype(jnp.bfloat16)
    upstream = cotangent.astype(jnp.float32)
    grad_normed, grad_paired, grad_router, grad_mixer, grad_constant = pull_mix(upstream)
    pair_grads = grad_paired.astype(jnp.bfloat16).reshape(token_count * width_top, D)
    outgoing_grad = jnp.take(pair_grads, owners, axis=0, mode="fill", fill_value=0)
    arrived_grad = lax.all_to_all(
        outgoing_grad.reshape(groups, local_experts * capacity, D),
        "expert",
        split_axis=0,
        concat_axis=0,
        tiled=True,
    )
    arrived_grad = arrived_grad.reshape(groups, local_experts, capacity, D)
    sigmoid_gate = jax.nn.sigmoid(gate_part)
    grad_active = jnp.einsum(
        "secd,efd->secf", arrived_grad, expert_outer, preferred_element_type=jnp.float32
    )
    grad_gate = grad_active * up_part * sigmoid_gate * (1.0 + gate_part * (1.0 - sigmoid_gate))
    grad_up = grad_active * gate_part * sigmoid_gate
    grad_joined = jnp.concatenate([grad_gate, grad_up], axis=-1).astype(jnp.bfloat16)
    grad_rows = jnp.einsum(
        "secf,edf->secd", grad_joined, expert_inner, preferred_element_type=jnp.float32
    ).astype(jnp.bfloat16)
    grad_returned = lax.all_to_all(
        grad_rows.reshape(groups, local_experts * capacity, D),
        "expert",
        split_axis=0,
        concat_axis=0,
        tiled=True,
    )
    grad_slots = jnp.take(
        grad_returned.reshape(experts * capacity, D), targets, axis=0, mode="fill", fill_value=0
    ).astype(jnp.float32)
    grad_normed = grad_normed + jnp.sum(grad_slots, axis=1)
    grad_middle_norm, grad_gain_second = pull_second(grad_normed)
    grad_middle = upstream + grad_middle_norm
    grad_attention = grad_middle.astype(jnp.bfloat16)
    grad_weight_out = jnp.einsum(
        "td,te->de", attended_flat, grad_attention, preferred_element_type=jnp.float32
    )
    grad_attended = jnp.einsum(
        "te,de->td", grad_attention, weight_out, preferred_element_type=jnp.float32
    ).astype(jnp.bfloat16)
    grad_attended = grad_attended.reshape(SEQS_DEV, SEQ, HEADS, HEAD_DIM)
    grad_packed = lax.map(
        attend_backward, (queries, key_rows, value_rows, segments, logsums, grad_attended)
    )
    grad_packed = grad_packed.reshape(token_count, 3 * D).astype(jnp.bfloat16)
    grad_weight_in = jnp.einsum(
        "td,tf->df", normed_first, grad_packed, preferred_element_type=jnp.float32
    )
    grad_normed_first = jnp.einsum(
        "tf,df->td", grad_packed, weight_in, preferred_element_type=jnp.float32
    )
    grad_hidden_norm, grad_gain_first = pull_first(grad_normed_first)
    input_grad = grad_middle + grad_hidden_norm
    grad_gains = jnp.stack([grad_gain_first, grad_gain_second], axis=0)
    grad_outer = jnp.einsum(
        "secf,secd->efd", activated, arrived_grad, preferred_element_type=jnp.float32
    )
    grad_inner = jnp.einsum(
        "secd,secf->edf", slot_rows, grad_joined, preferred_element_type=jnp.float32
    )
    grad_inner_own, grad_outer_own = (
        lax.psum_scatter(grad_inner, "dp", scatter_dimension=1, tiled=True),
        lax.psum_scatter(grad_outer, "dp", scatter_dimension=1, tiled=True),
    )
    dense_terms = (grad_weight_in, grad_weight_out, grad_router, grad_constant, grad_gains)
    dense_own = (
        lax.psum_scatter(dense_terms[0], ("dp", "expert"), scatter_dimension=0, tiled=True),
        lax.psum_scatter(dense_terms[1], ("dp", "expert"), scatter_dimension=0, tiled=True),
        lax.psum_scatter(dense_terms[2], ("dp", "expert"), scatter_dimension=0, tiled=True),
        lax.psum_scatter(dense_terms[3], ("dp", "expert"), scatter_dimension=0, tiled=True),
        lax.psum_scatter(dense_terms[4], ("dp", "expert"), scatter_dimension=1, tiled=True),
    )
    owned_grads = tuple(dense_own) + (grad_inner_own, grad_outer_own)
    partial_square = sum((jnp.sum(member * member) for member in owned_grads))
    square_total, mixer_total = lax.psum((partial_square, grad_mixer), ("dp", "expert"))
    grad_norm = jnp.sqrt(square_total + jnp.sum(mixer_total * mixer_total))
    factor = clip_limit / jnp.maximum(grad_norm, clip_limit)
    results = (activations, input_grad, grad_norm)
    results = results + adam_step(
        attend_in, first_attend_in, second_attend_in, dense_own[0], factor, learn_rates[0]
    )
    results = results + adam_step(
        attend_out, first_attend_out, second_attend_out, dense_own[1], factor, learn_rates[1]
    )
    results = results + adam_step(
        router, first_router, second_router, dense_own[2], factor, learn_rates[2]
    )
    results = results + adam_step(
        gate_mix, first_gate_mix, second_gate_mix, mixer_total, factor, learn_rates[3]
    )
    results = results + adam_step(
        constants, first_constants, second_constants, dense_own[3], factor, learn_rates[4]
    )
    results = results + adam_step(
        norm_gains, first_norm_gains, second_norm_gains, dense_own[4], factor, learn_rates[5]
    )
    results = results + adam_step(
        expert_in, first_expert_in, second_expert_in, grad_inner_own, factor, learn_rates[6]
    )
    results = results + adam_step(
        expert_out, first_expert_out, second_expert_out, grad_outer_own, factor, learn_rates[7]
    )
    return results


def solution(mesh):
    in_specs = (
        P(("dp", "expert"), None),
        P(("dp", "expert"), None),
        P(("dp", "expert"), None),
        P(("dp", "expert"), None),
        P(("dp", "expert"), None),
        P(("dp", "expert"), None),
        P(("dp", "expert"), None),
        P(("dp", "expert"), None),
        P(("dp", "expert"), None),
        P(("dp", "expert"), None),
        P(("dp", "expert"), None),
        P(("dp", "expert"), None),
        P(("dp", "expert"), None),
        P(("dp", "expert"), None),
        P(("dp", "expert"), None),
        P(),
        P(),
        P(),
        P(("dp", "expert"), None),
        P(("dp", "expert"), None),
        P(("dp", "expert"), None),
        P(None, ("dp", "expert")),
        P(None, ("dp", "expert")),
        P(None, ("dp", "expert")),
        P("expert", "dp", None),
        P("expert", "dp", None),
        P("expert", "dp", None),
        P("expert", "dp", None),
        P("expert", "dp", None),
        P("expert", "dp", None),
    )
    out_specs = (
        P(("dp", "expert"), None),
        P(("dp", "expert"), None),
        P(),
        P(("dp", "expert"), None),
        P(("dp", "expert"), None),
        P(("dp", "expert"), None),
        P(("dp", "expert"), None),
        P(("dp", "expert"), None),
        P(("dp", "expert"), None),
        P(("dp", "expert"), None),
        P(("dp", "expert"), None),
        P(("dp", "expert"), None),
        P(("dp", "expert"), None),
        P(("dp", "expert"), None),
        P(("dp", "expert"), None),
        P(("dp", "expert"), None),
        P(("dp", "expert"), None),
        P(("dp", "expert"), None),
        P(),
        P(),
        P(),
        P(),
        P(),
        P(("dp", "expert"), None),
        P(("dp", "expert"), None),
        P(("dp", "expert"), None),
        P(("dp", "expert"), None),
        P(("dp", "expert"), None),
        P(None, ("dp", "expert")),
        P(None, ("dp", "expert")),
        P(None, ("dp", "expert")),
        P(None, ("dp", "expert")),
        P(None, ("dp", "expert")),
        P("expert", "dp", None),
        P("expert", "dp", None),
        P("expert", "dp", None),
        P("expert", "dp", None),
        P("expert", "dp", None),
        P("expert", "dp", None),
        P("expert", "dp", None),
        P("expert", "dp", None),
        P("expert", "dp", None),
        P("expert", "dp", None),
    )
    return jax.shard_map(body, mesh=mesh, in_specs=in_specs, out_specs=out_specs, check_vma=False)
```

profile of v0, /device:TPU:0, one launch (start us, length us, event | category | flops | bytes accessed | tf_op | source)
XLA Modules:
  0.0 1191.3 jit_solution(14105542134507167650)
XLA Ops:
  17.7 12.5 %gather_fusion.3 = f32[2048]{0:T(1024)S(1)} fusion(f32[1024,8]{0,1:T(8,128)S(1)} %fusion.62, s32[2048]{0:T(1024)S(1)} %reshape.474), kind=kCustom, calls=%fused_computation.5 | custom fusion | bytes 32768 | tf_op jit(solution)/shard_map/jit(take_along_axis)/gather | solution.py:38
  31.5 8.0 scatter_custom_fusion
  40.5 43.1 %all-gather = bf16[32,24,2]{1,2,0:T(2,128)(2,1)S(1)} all-gather(bf16[1,24,2]{1,2,0:T(2,128)(2,1)S(1)} %convert_bitcast_fusion.2), channel_id=1, replica_groups=mesh['dp'=8,'expert'=4] {'dp','expert'}, dimensions={0}, use_global_device_ids=true | all-gather | bytes 3168 | tf_op jit(solution)/shard_map/all_gather | solution.py:172
  83.8 36.9 %all-gather.2 = bf16[32,24,6]{1,2,0:T(8,128)(2,1)S(1)} all-gather(bf16[1,24,6]{1,2,0:T(8,128)(2,1)S(1)} %convert_bitcast_fusion), channel_id=1, replica_groups=mesh['dp'=8,'expert'=4] {'dp','expert'}, dimensions={0}, use_global_device_ids=true | all-gather | bytes 9504 | tf_op jit(solution)/shard_map/all_gather | solution.py:171
  121.4 38.6 %all-gather.1 = bf16[32,24,8]{1,2,0:T(8,128)(2,1)S(1)} all-gather(bf16[1,24,8]{1,2,0:T(8,128)(2,1)S(1)} %convert_bitcast_fusion.1), channel_id=1, replica_groups=mesh['dp'=8,'expert'=4] {'dp','expert'}, dimensions={0}, use_global_device_ids=true | all-gather | bytes 12672 | tf_op jit(solution)/shard_map/all_gather | solution.py:170
  170.5 7.8 convolution_convert_fusion
  185.0 21.6 %fusion.3 = (f32[12,1024]{1,0:T(8,128)S(1)}, f32[12,1024,1024]{1,2,0:T(8,128)}) fusion(pred[1024,1024]{0,1:T(8,128)(4,1)S(1)} %fusion.61, bf16[1,1024,3,12,64]{1,4,3,2,0:T(8,128)(2,1)} %bitcast.218), kind=kOutput, calls=%fused_computation.16 | convolution fusion | flops 1648349184 | bytes 54575104 | tf_op jit(solution)/shard_map/while/body/eval_jaxpr/qhd,khd->hqk/dot_general | solution.py:74
  206.6 21.1 %exponential_reduce_fusion = f32[12,1024]{1,0:T(8,128)S(1)} fusion(f32[12,1024,1024]{1,2,0:T(8,128)} %get-tuple-element.485, f32[12,1024]{1,0:T(8,128)S(1)} %get-tuple-element.484, pred[1024,1024]{0,1:T(8,128)(4,1)S(1)} %fusion.61), kind=kLoop, calls=%fused_computation.14 | loop fusion | flops 50319360 | bytes 51478528 | tf_op jit(solution)/shard_map/while/body/eval_jaxpr/reduce_sum | solution.py:86
  228.3 21.0 %convolution_convert_fusion.3 = bf16[12,64,1024]{2,1,0:T(8,128)(2,1)} fusion(bf16[1,1024,3,12,64]{1,4,3,2,0:T(8,128)(2,1)} %bitcast.219, f32[12,1024,1024]{1,2,0:T(8,128)} %get-tuple-element.485, f32[12,1024]{1,0:T(8,128)S(1)} %log_add_fusion, pred[1024,1024]{0,1:T(8,128)(4,1)S(1)} %fusion.61), kind=kOutput, calls=%fused_computation.157 | convolution fusion | flops 1661730816 | bytes 54575104 | tf_op jit(solution)/shard_map/while/body/eval_jaxpr/hqk,khd->qhd/dot_general | solution.py:89
  257.5 12.5 %gather_fusion.2 = f32[2048]{0:T(1024)S(1)} fusion(f32[1024,8]{0,1:T(8,128)S(1)} %fusion.149, s32[2048]{0:T(1024)S(1)} %reshape.474), kind=kCustom, calls=%fused_computation.4 | custom fusion | bytes 32768 | tf_op jit(solution)/shard_map/jvp(jit(take_along_axis))/gather | solution.py:52
  308.0 12.5 %convolution_bitcast_fusion = f32[4,1,256,4096]{3,2,0,1:T(8,128)} fusion(bf16[4,256,768]{2,1,0:T(8,128)(2,1)} %all-to-all-done, bf16[1,768,4096]{2,1,0:T(8,128)(2,1)} %all-gather.12.cloned.1.call-done), kind=kOutput, calls=%fused_computation.36 | convolution fusion | flops 6442450944 | bytes 24641536 | tf_op jit(solution)/shard_map/secd,edf->secf/dot_general | solution.py:207
  328.0 15.0 %fusion.65 = (bf16[4,256,2048]{2,1,0:T(8,128)(2,1)}, bf16[4,256,2048]{2,1,0:T(8,128)(2,1)}, bf16[4,1,256,2048]{3,2,0,1:T(8,128)(2,1)S(1)}) fusion(f32[4,1,256,4096]{3,2,0,1:T(8,128)} %convolution_bitcast_fusion, bf16[4,256,768]{2,1,0:T(8,128)(2,1)S(1)} %all-to-all-done.2, bf16[1,2048,768]{2,1,0:T(8,128)(2,1)} %all-gather.14.cloned.1.call-done), kind=kOutput, calls=%fused_computation.97 | convolution fusion | flops 3254779904 | bytes 34078720 | tf_op jit(solution)/shard_map/secd,efd->secf/dot_general | solution.py:252
  353.0 11.9 fusion.117
  364.9 8.2 all-to-all-done.1
  378.6 9.8 gather_fusion.4
  395.7 8.7 copy.333
  404.3 9.4 gather_fusion.5
  419.9 11.1 convert_reduce_fusion
  437.9 10.1 fusion.104
  450.5 11.4 scatter_custom_fusion.1
  481.1 21.2 %fusion.126 = bf16[1024,1,12,64]{0,3,2,1:T(8,128)(2,1)} fusion(bf16[1024,12,64]{0,2,1:T(8,128)(2,1)S(1)} %bitcast.227, f32[12,1024,1024]{1,2,0:T(8,128)} %get-tuple-element.485, f32[12,1024]{1,0:T(8,128)S(1)} %copy-done.55, pred[1024,1024]{0,1:T(8,128)(4,1)S(1)} %copy-done.11), kind=kOutput, calls=%fused_computation.166 | convolution fusion | flops 1661730816 | bytes 54575104 | tf_op jit(solution)/shard_map/while/body/eval_jaxpr/hqk,qhd->khd/dot_general | solution.py:100
  502.4 21.6 %fusion.133 = f32[12,1024,1024]{1,2,0:T(8,128)} fusion(bf16[1024,12,64]{0,2,1:T(8,128)(2,1)} %bitcast.228, bf16[1,1024,3,12,64]{1,4,3,2,0:T(8,128)(2,1)} %bitcast.220), kind=kOutput, calls=%fused_computation.169 | convolution fusion | flops 1610612736 | bytes 53477376 | tf_op jit(solution)/shard_map/while/body/eval_jaxpr/qhd,khd->hqk/dot_general | solution.py:97
  523.9 66.1 %fusion.130 = bf16[1024,1,12,64]{0,3,2,1:T(8,128)(2,1)} fusion(f32[12,1024,1024]{1,2,0:T(8,128)} %fusion.133, f32[12,1024,1024]{1,2,0:T(8,128)} %get-tuple-element.485, f32[12,1024]{1,0:T(8,128)S(1)} %copy-done.55, pred[1024,1024]{0,1:T(8,128)(4,1)} %copy-done.10, bf16[1,1024,3,12,64]{1,4,3,2,0:T(8,128)(2,1)} %bitcast.221), kind=kOutput, calls=%fused_computation.168 | convolution fusion | flops 1749824512 | bytes 206700544 | tf_op jit(solution)/shard_map/while/body/eval_jaxpr/hqk,khd->qhd/dot_general | solution.py:108
  590.1 66.9 %fusion.127 = bf16[1024,1,12,64]{0,3,2,1:T(8,128)(2,1)} fusion(f32[12,1024,1024]{1,2,0:T(8,128)} %fusion.133, f32[12,1024,1024]{1,2,0:T(8,128)} %get-tuple-element.485, f32[12,1024]{1,0:T(8,128)S(1)} %copy-done.55, pred[1024,1024]{0,1:T(8,128)(4,1)} %copy-done.10, bf16[1,1024,3,12,64]{1,4,3,2,0:T(8,128)(2,1)} %bitcast.222), kind=kOutput, calls=%fused_computation.167 | convolution fusion | flops 1749824512 | bytes 206700544 | tf_op jit(solution)/shard_map/while/body/eval_jaxpr/hqk,qhd->khd/dot_general | solution.py:111
  668.1 8.8 fusion.66
  677.1 14.1 %convolution_bitcast_fusion.1 = f32[1,768,4096]{2,1,0:T(8,128)} fusion(bf16[4,256,768]{2,1,0:T(8,128)(2,1)} %all-to-all-done, bf16[4,256,2048]{2,1,0:T(8,128)(2,1)} %get-tuple-element.470, bf16[4,256,2048]{2,1,0:T(8,128)(2,1)} %get-tuple-element.469), kind=kOutput, calls=%fused_computation.47 | convolution fusion | flops 6459228160 | bytes 22544384 | tf_op jit(solution)/shard_map/secd,secf->edf/dot_general | solution.py:298
  702.1 9.5 fusion.72
  714.3 39.7 %all-reduce.21 = (f32[768,8]{0,1:T(8,128)S(1)}, f32[768,6]{0,1:T(8,128)S(1)}, f32[2,768]{1,0:T(2,128)S(1)}) all-reduce(f32[768,8]{0,1:T(8,128)S(1)} %fusion.211, f32[768,6]{0,1:T(8,128)S(1)} %pad_add_fusion, f32[2,768]{1,0:T(2,128)S(1)} %pad_maximum_fusion.6), channel_id=4, replica_groups=mesh['dp'=8,'expert'=4] {'dp','expert'}, use_global_device_ids=true, to_apply=%region_31.33.clone | all-reduce | flops 12288 | bytes 98304
  763.5 22.6 %reduce-scatter.8.cloned.1.call-done = f32[24,2304]{1,0:T(8,128)} async-done(((f32[768,2304]{1,0:T(8,128)}), f32[24,2304]{1,0:T(8,128)}) %reduce-scatter.8.cloned.1.call-update) | async-done | bytes 221200 | tf_op jit(solution)/shard_map/reduce_scatter | solution.py:307
  791.0 116.5 %reduce-scatter.14.cloned.1.call-done = f32[1,256,768]{2,1,0:T(8,128)} async-done(((f32[1,2048,768]{2,1,0:T(8,128)}), f32[1,256,768]{2,1,0:T(8,128)}) %reduce-scatter.14.cloned.1.call-update) | async-done | bytes 786448 | tf_op jit(solution)/shard_map/reduce_scatter | solution.py:303
  909.4 208.7 %reduce-scatter.12.cloned.1.call-done = f32[1,96,4096]{2,1,0:T(8,128)} async-done(((f32[1,768,4096]{2,1,0:T(8,128)}), f32[1,96,4096]{2,1,0:T(8,128)}) %reduce-scatter.12.cloned.1.call-update) | async-done | bytes 1572880 | tf_op jit(solution)/shard_map/reduce_scatter | solution.py:302
  1125.7 39.4 %all-reduce.20 = (f32[]{:T(128)}, f32[8,8]{0,1:T(8,128)S(1)}) all-reduce(f32[]{:T(128)S(6)} %add.365, f32[8,8]{0,1:T(8,128)S(1)} %convolution_bitcast_fusion.2), channel_id=1, replica_groups=mesh['dp'=8,'expert'=4] {'dp','expert'}, use_global_device_ids=true, to_apply=%region_47.49 | all-reduce | flops 65 | bytes 520 | tf_op jit(solution)/shard_map/psum | solution.py:315
  (397 shorter events, 201.8 us)
Async XLA Ops:
  7.2 163.1 %copy-start = (f32[1024,8]{0,1:T(8,128)S(1)}, f32[1024,8]{0,1:T(8,128)}, u32[]{:S(2)}) copy-start(f32[1024,8]{0,1:T(8,128)} %param.33) | copy-start | bytes 98308
  7.3 163.2 %all-gather.8.cloned.1.call-start = ((), (), s32[]{:S(2)}) async-start(), calls=%async_computation.8 | async-start | bytes 3649536 | tf_op jit(solution)/shard_map/all_gather | solution.py:168
  9.0 240.4 %all-gather.10.cloned.1.call-start = ((), (), s32[]{:S(2)}) async-start(), calls=%async_computation.9 | async-start | bytes 1216512 | tf_op jit(solution)/shard_map/all_gather | solution.py:169
  10.6 297.4 %all-gather.12.cloned.1.call-start = ((), (), s32[]{:S(2)}) async-start(), calls=%async_computation.10 | async-start | bytes 7077888 | tf_op jit(solution)/shard_map/all_gather | solution.py:175
  13.0 307.5 %all-gather.14.cloned.1.call-start = ((), (), s32[]{:S(2)}) async-start(), calls=%async_computation.11 | async-start | bytes 3538944 | tf_op jit(solution)/shard_map/all_gather | solution.py:176
  30.2 134.3 %copy-start.71 = (s32[1,1024]{1,0:T(1,128)S(1)}, s32[1,1024]{1,0:T(1,128)}, u32[]{:S(2)}) copy-start(s32[1,1024]{1,0:T(1,128)} %param.36) | copy-start | bytes 12292
  30.9 133.6 %copy-start.66 = (pred[1024,2]{0,1:T(4,128)(4,1)}, pred[1024,2]{0,1:T(4,128)(4,1)S(1)}, u32[]{:S(2)}) copy-start(pred[1024,2]{0,1:T(4,128)(4,1)S(1)} %get-tuple-element.467) | copy-start | bytes 6148
  83.7 86.8 %copy-start.72 = (f32[768]{0:T(1024)}, f32[768]{0:T(1024)S(1)}, u32[]{:S(2)}) copy-start(f32[768]{0:T(1024)S(1)} %get-tuple-element.421) | copy-start | bytes 9220
  83.8 169.1 %copy-start.45 = (f32[768]{0:T(1024)}, f32[768]{0:T(1024)S(1)}, u32[]{:S(2)}) copy-start(f32[768]{0:T(1024)S(1)} %get-tuple-element.420) | copy-start | bytes 9220
  160.2 96.3 %copy-start.56 = (bf16[768,8]{0,1:T(8,128)(2,1)}, bf16[768,8]{0,1:T(8,128)(2,1)S(1)}, u32[]{:S(2)}) copy-start(bf16[768,8]{0,1:T(8,128)(2,1)S(1)} %reshape.509) | copy-start | bytes 36868
  165.1 62.6 %copy-start.10 = (pred[1024,1024]{0,1:T(8,128)(4,1)}, pred[1024,1024]{0,1:T(8,128)(4,1)S(1)}, u32[]{:S(2)}) copy-start(pred[1024,1024]{0,1:T(8,128)(4,1)S(1)} %fusion.61) | copy-start | bytes 3145732
  167.2 82.2 %copy-start.12 = (bf16[1024,768]{0,1:T(8,128)(2,1)}, bf16[1024,768]{0,1:T(8,128)(2,1)S(1)}, u32[]{:S(2)}) copy-start(bf16[1024,768]{0,1:T(8,128)(2,1)S(1)} %copy.322) | copy-start | bytes 4718596
  278.2 26.1 %all-to-all-start = ((bf16[4,256,768]{2,1,0:T(8,128)(2,1)}), bf16[4,256,768]{2,1,0:T(8,128)(2,1)}, u32[]{:S(2)}, u32[]{:S(2)}) async-start(bf16[4,256,768]{2,1,0:T(8,128)(2,1)} %broadcast_select_fusion.2), calls=%async_computation | async-start | bytes 3145728 | tf_op jit(solution)/shard_map/all_to_all | solution.py:199
  304.2 23.8 %all-to-all-start.2 = ((bf16[4,256,768]{2,1,0:T(8,128)(2,1)}), bf16[4,256,768]{2,1,0:T(8,128)(2,1)S(1)}, u32[]{:S(2)}, u32[]{:S(2)}) async-start(bf16[4,256,768]{2,1,0:T(8,128)(2,1)} %broadcast_select_fusion.1), calls=%async_computation.2 | async-start | bytes 3145728 | tf_op jit(solution)/shard_map/all_to_all | solution.py:243
  349.4 23.6 %all-to-all-start.1 = ((bf16[4,256,768]{2,1,0:T(8,128)(2,1)}), bf16[4,256,768]{2,1,0:T(8,128)(2,1)S(1)}, u32[]{:S(2)}, u32[]{:S(2)}) async-start(bf16[4,256,768]{2,1,0:T(8,128)(2,1)} %fusion.120), calls=%async_computation.1 | async-start | bytes 3145728 | tf_op jit(solution)/shard_map/all_to_all | solution.py:216
  373.0 31.3 %all-to-all-start.3 = ((bf16[4,256,768]{2,1,0:T(8,128)(2,1)}), bf16[4,256,768]{2,1,0:T(8,128)(2,1)S(1)}, u32[]{:S(2)}, u32[]{:S(2)}) async-start(bf16[4,256,768]{2,1,0:T(8,128)(2,1)} %fusion.117), calls=%async_computation.3 | async-start | bytes 3145728 | tf_op jit(solution)/shard_map/all_to_all | solution.py:261
  376.6 385.4 %reduce-scatter.10.cloned.1.call-start = ((), (), s32[]{:S(2)}) async-start(), calls=%async_computation.13 | async-start | bytes 2433024 | tf_op jit(solution)/shard_map/reduce_scatter | solution.py:308
  378.6 58.6 %copy-start.62 = (f32[1024,1,1]{0,2,1:T(1,128)}, f32[1024,1,1]{0,2,1:T(1,128)S(1)}, u32[]{:S(2)}) copy-start(f32[1024,1,1]{0,2,1:T(1,128)S(1)} %get-tuple-element.475) | copy-start | bytes 12292
  378.6 58.6 %copy-start.64 = (f32[1024,1,1]{0,2,1:T(1,128)}, f32[1024,1,1]{0,2,1:T(1,128)S(1)}, u32[]{:S(2)}) copy-start(f32[1024,1,1]{0,2,1:T(1,128)S(1)} %get-tuple-element.477) | copy-start | bytes 12292
  476.2 309.9 %reduce-scatter.8.cloned.1.call-start = ((), (), s32[]{:S(2)}) async-start(), calls=%async_computation.12 | async-start | bytes 7299072 | tf_op jit(solution)/shard_map/reduce_scatter | solution.py:307
  668.1 239.4 %reduce-scatter.14.cloned.1.call-start = ((), (), s32[]{:S(2)}) async-start(), calls=%async_computation.15 | async-start | bytes 7077888 | tf_op jit(solution)/shard_map/reduce_scatter | solution.py:303
  677.0 441.1 %reduce-scatter.12.cloned.1.call-start = ((), (), s32[]{:S(2)}) async-start(), calls=%async_computation.14 | async-start | bytes 14155776 | tf_op jit(solution)/shard_map/reduce_scatter | solution.py:302
  755.9 416.5 %copy-start.88 = (f32[24,8]{0,1:T(8,128)}, f32[24,8]{0,1:T(8,128)S(1)}, u32[]{:S(2)}) copy-start(f32[24,8]{0,1:T(8,128)S(1)} %get-tuple-element.464) | copy-start | bytes 2308
  756.5 415.2 %copy-start.89 = (f32[24,6]{0,1:T(8,128)}, f32[24,6]{0,1:T(8,128)S(1)}, u32[]{:S(2)}) copy-start(f32[24,6]{0,1:T(8,128)S(1)} %get-tuple-element.462) | copy-start | bytes 1732
  1121.9 51.9 %copy-start.32 = (f32[24,768]{1,0:T(8,128)S(1)}, f32[24,768]{1,0:T(8,128)}, u32[]{:S(2)}) copy-start(f32[24,768]{1,0:T(8,128)} %param.41) | copy-start | bytes 221188
  1121.9 53.4 %copy-start.26 = (f32[24,2304]{1,0:T(8,128)S(1)}, f32[24,2304]{1,0:T(8,128)}, u32[]{:S(2)}) copy-start(f32[24,2304]{1,0:T(8,128)} %reduce-scatter.8.cloned.1.call-done) | copy-start | bytes 663556
  1121.9 53.4 %copy-start.27 = (f32[24,2304]{1,0:T(8,128)S(1)}, f32[24,2304]{1,0:T(8,128)}, u32[]{:S(2)}) copy-start(f32[24,2304]{1,0:T(8,128)} %param.38) | copy-start | bytes 663556
  1122.0 53.4 %copy-start.39 = (f32[24,2304]{1,0:T(8,128)S(1)}, f32[24,2304]{1,0:T(8,128)}, u32[]{:S(2)}) copy-start(f32[24,2304]{1,0:T(8,128)} %param.39) | copy-start | bytes 663556
  1122.0 53.4 %copy-start.40 = (f32[24,2304]{1,0:T(8,128)S(1)}, f32[24,2304]{1,0:T(8,128)}, u32[]{:S(2)}) copy-start(f32[24,2304]{1,0:T(8,128)} %param.40) | copy-start | bytes 663556
  1122.0 54.4 %copy-start.20 = (f32[1,256,768]{2,1,0:T(8,128)S(1)}, f32[1,256,768]{2,1,0:T(8,128)}, u32[]{:S(2)}) copy-start(f32[1,256,768]{2,1,0:T(8,128)} %param.59) | copy-start | bytes 2359300
  1122.0 54.4 %copy-start.21 = (f32[1,256,768]{2,1,0:T(8,128)S(1)}, f32[1,256,768]{2,1,0:T(8,128)}, u32[]{:S(2)}) copy-start(f32[1,256,768]{2,1,0:T(8,128)} %reduce-scatter.14.cloned.1.call-done) | copy-start | bytes 2359300
  1122.0 54.4 %copy-start.30 = (f32[1,256,768]{2,1,0:T(8,128)S(1)}, f32[1,256,768]{2,1,0:T(8,128)}, u32[]{:S(2)}) copy-start(f32[1,256,768]{2,1,0:T(8,128)} %param.60) | copy-start | bytes 2359300
  (92 other events, 958.4 us)
Sparse Core Ops, SparseCore 0:
  11.6 62.7 all-gather.7
  77.9 52.8 all-gather.9
  133.6 97.9 all-gather.11
  234.2 58.6 all-gather.13
  476.3 96.7 reduce-scatter.9
  668.2 117.8 reduce-scatter.7
  790.3 117.1 reduce-scatter.13
  911.6 206.4 reduce-scatter.11
where the time goes:
time: 1200 us; the launch traced here: 1190 us
  waiting for transfers between devices  364 us (30%)
  matrix products  334 us (28%)
  blocking collectives  198 us (16%)
  local copies, waits for them, and re-layouts  146 us (12%)
  other arithmetic  112 us (9%)
  between operations  23.2 us (2%)
  starting transfers between devices  15.6 us (1%)
    reduce_scatter x1, waiting for transfers between devices, body(): lax.psum_scatter(grad_inner, 'dp', scatter_dimension=1, tiled=True)  209 us
    reduce_scatter x1, waiting for transfers between devices, body(): lax.psum_scatter(grad_outer, 'dp', scatter_dimension=1, tiled=True)  116 us
    dot_general x1, matrix products, attend_backward(): jnp.einsum('hqk,qhd->khd', grad_raw, queries, preferred_element_type=jnp....  66.9 us
    dot_general x1, matrix products, attend_backward(): jnp.einsum('hqk,khd->qhd', grad_raw, key_rows, preferred_element_type=jnp...  66.1 us
    all_gather x1, blocking collectives, body(): lax.all_gather(norm_gains.astype(jnp.bfloat16), ('dp', 'expert'), axis=1,...  43.1 us
    unnamed x1, blocking collectives  39.7 us
    psum x1, blocking collectives, body(): lax.psum((partial_square, grad_mixer), ('dp', 'expert'))  39.4 us
    all_gather x1, blocking collectives, body(): lax.all_gather(router.astype(jnp.bfloat16), ('dp', 'expert'), axis=0, til...  38.6 us
  transfers between devices with their start and end apart: 12, of which 5 were waited for; matrix products, arithmetic and copies ran while one was open for 39% of the time, Pallas kernels for 0%

commit v1 on v0

v1 whole, which is shorter than its diff:
```python
import functools

import jax
import jax.numpy as jnp
from jax import lax
from jax.experimental import pallas as pl
from jax.experimental.pallas import tpu as pltpu
from jax.sharding import PartitionSpec as P

D = 768
FF = 2048
HEAD_DIM = 64
PAIR = 2 * HEAD_DIM
BLOCK = 256
LANES = 128
BOTH = ("dp", "expert")

norm_epsilon = 1e-05
adam_epsilon = 1e-08
learn_rates = (0.01, 0.04, 0.01, 0.03, 0.01, 0.1, 0.01, 0.01)
decay_rate = 0.1
beta_moment = 0.5
step_number = 4.0
clip_limit = 1.0
score_scale = 0.125
masked_score = -1e30
highest = lax.Precision.HIGHEST
F32 = jnp.float32
BF16 = jnp.bfloat16

NN = (((1,), (0,)), ((), ()))
NT = (((1,), (1,)), ((), ()))
TN = (((0,), (0,)), ((), ()))

CHOSEN, COEF, SCALE, REST, BETA, GATE_GRAD, PROBS = 0, 2, 3, 4, 8, 16, 32


def dot(left, right, form=NN):
    return lax.dot_general(left, right, form, preferred_element_type=F32)


def iota(shape, dim):
    return lax.broadcasted_iota(jnp.int32, shape, dim)


def row_scale(values):
    return lax.rsqrt(jnp.mean(values * values, axis=-1, keepdims=True) + norm_epsilon)


def params(mebibytes):
    return pltpu.CompilerParams(vmem_limit_bytes=mebibytes << 20)


def whole(shape):
    return pl.BlockSpec(shape, lambda *step: (0,) * len(shape))


def cost(flops, moved, transcendentals=0):
    return pl.CostEstimate(flops=flops, bytes_accessed=moved, transcendentals=transcendentals)


def project_kernel(hidden_ref, gain_ref, weight_ref, normed_ref, packed_ref):
    @pl.when(pl.program_id(0) == 0)
    def _():
        values = hidden_ref[...].astype(F32)
        normed_ref[...] = (values * row_scale(values) * gain_ref[...]).astype(BF16)

    packed_ref[...] = dot(normed_ref[...], weight_ref[...]).astype(BF16)


def project(hidden, gain, weights):
    tokens = hidden.shape[0]
    return pl.pallas_call(
        project_kernel,
        grid=(3,),
        in_specs=[
            whole((tokens, D)),
            whole((1, D)),
            pl.BlockSpec((D, D), lambda step: (0, step)),
        ],
        out_specs=[whole((tokens, D)), pl.BlockSpec((tokens, D), lambda step: (0, step))],
        out_shape=[
            jax.ShapeDtypeStruct((tokens, D), BF16),
            jax.ShapeDtypeStruct((tokens, 3 * D), BF16),
        ],
        compiler_params=params(40),
        cost_estimate=cost(6 * tokens * D * D, 10 * tokens * D + 6 * D * D),
        name="project",
    )(hidden, gain, weights)


def attend_forward_kernel(
    query_ref, key_ref, value_ref, seg_column_ref, seg_row_ref, out_ref, logsum_ref, bias_ref, *, block
):
    length = query_ref.shape[0]

    @pl.when(pl.program_id(0) == 0)
    def _():
        for low in range(0, length, block):
            high = low + block
            rows = low + iota((block, high), 0)
            allowed = jnp.logical_and(
                seg_column_ref[low:high, :] == seg_row_ref[:, :high], iota((block, high), 1) <= rows
            )
            bias_ref[low:high, :high] = jnp.where(allowed, 0.0, masked_score)

    for low in range(0, length, block):
        high = low + block
        for head in range(2):
            lanes = slice(head * HEAD_DIM, (head + 1) * HEAD_DIM)
            queries = query_ref[low:high, lanes] * score_scale
            scores = dot(queries, key_ref[:high, lanes], NT) + bias_ref[low:high, :high]
            maximum = jnp.max(scores, axis=1, keepdims=True)
            powers = jnp.exp(scores - maximum)
            totals = jnp.sum(powers, axis=1, keepdims=True)
            weights = (powers * (1.0 / totals)).astype(BF16)
            out_ref[low:high, lanes] = dot(weights, value_ref[:high, lanes]).astype(BF16)
            logsum_ref[0, low:high, head : head + 1] = maximum + jnp.log(totals)


def attend_forward(packed, seg_column, seg_row):
    length = packed.shape[0]
    pairs = D // PAIR
    return pl.pallas_call(
        functools.partial(attend_forward_kernel, block=2 * BLOCK),
        grid=(pairs,),
        in_specs=[
            pl.BlockSpec((length, PAIR), lambda pair: (0, pair)),
            pl.BlockSpec((length, PAIR), lambda pair: (0, pairs + pair)),
            pl.BlockSpec((length, PAIR), lambda pair: (0, 2 * pairs + pair)),
            whole((length, 1)),
            whole((1, length)),
        ],
        out_specs=[
            pl.BlockSpec((length, PAIR), lambda pair: (0, pair)),
            pl.BlockSpec((1, length, 2), lambda pair: (pair, 0, 0)),
        ],
        out_shape=[
            jax.ShapeDtypeStruct((length, D), BF16),
            jax.ShapeDtypeStruct((pairs, length, 2), F32),
        ],
        scratch_shapes=[pltpu.VMEM((length, length), F32)],
        compiler_params=params(48),
        cost_estimate=cost(8 * length * length * D, 8 * length * D, length * length * 8),
        name="attend_forward",
    )(packed, packed, packed, seg_column, seg_row)


def attend_backward_kernel(
    query_ref,
    key_ref,
    value_ref,
    grad_ref,
    logsum_ref,
    seg_column_ref,
    seg_row_ref,
    out_ref,
    bias_ref,
    key_sum,
    value_sum,
    key_out,
    value_out,
    *,
    block,
):
    length = query_ref.shape[0]
    phase = pl.program_id(1)

    @pl.when(jnp.logical_and(pl.program_id(0) == 0, phase == 0))
    def _():
        for low in range(0, length, block):
            high = low + block
            columns = low + iota((high, block), 1)
            allowed = jnp.logical_and(
                seg_column_ref[:high, :] == seg_row_ref[:, low:high],
                iota((high, block), 0) <= columns,
            )
            bias_ref[:high, low:high] = jnp.where(allowed, 0.0, masked_score)

    @pl.when(phase == 0)
    def _():
        key_sum[...] = jnp.zeros_like(key_sum)
        value_sum[...] = jnp.zeros_like(value_sum)
        for low in range(0, length, block):
            high = low + block
            for head in range(2):
                lanes = slice(head * HEAD_DIM, (head + 1) * HEAD_DIM)
                queries = query_ref[low:high, lanes] * score_scale
                grads = grad_ref[low:high, lanes]
                keys = key_ref[:high, lanes]
                scores = dot(keys, queries, NT) + bias_ref[:high, low:high]
                weights = jnp.exp(scores - logsum_ref[0, head : head + 1, low:high])
                grad_weights = dot(value_ref[:high, lanes], grads, NT)
                value_sum[:high, lanes] += dot(weights.astype(BF16), grads)
                centred = jnp.sum(weights * grad_weights, axis=0, keepdims=True)
                grad_raw = (weights * (grad_weights - centred)).astype(BF16)
                key_sum[:high, lanes] += dot(grad_raw, queries)
                out_ref[low:high, lanes] = dot(grad_raw, keys * score_scale, TN).astype(BF16)
        key_out[...] = key_sum[...].astype(BF16)
        value_out[...] = value_sum[...].astype(BF16)

    @pl.when(phase == 1)
    def _():
        out_ref[...] = key_out[...]

    @pl.when(phase == 2)
    def _():
        out_ref[...] = value_out[...]


def attend_backward(packed, grad, logsum, seg_column, seg_row):
    length = packed.shape[0]
    pairs = D // PAIR
    return pl.pallas_call(
        functools.partial(attend_backward_kernel, block=2 * BLOCK),
        grid=(pairs, 3),
        in_specs=[
            pl.BlockSpec((length, PAIR), lambda pair, phase: (0, pair)),
            pl.BlockSpec((length, PAIR), lambda pair, phase: (0, pairs + pair)),
            pl.BlockSpec((length, PAIR), lambda pair, phase: (0, 2 * pairs + pair)),
            pl.BlockSpec((length, PAIR), lambda pair, phase: (0, pair)),
            pl.BlockSpec((1, 2, length), lambda pair, phase: (pair, 0, 0)),
            whole((length, 1)),
            whole((1, length)),
        ],
        out_specs=pl.BlockSpec((length, PAIR), lambda pair, phase: (0, phase * pairs + pair)),
        out_shape=jax.ShapeDtypeStruct((length, 3 * D), BF16),
        scratch_shapes=[
            pltpu.VMEM((length, length), F32),
            pltpu.VMEM((length, PAIR), F32),
            pltpu.VMEM((length, PAIR), F32),
            pltpu.VMEM((length, PAIR), BF16),
            pltpu.VMEM((length, PAIR), BF16),
        ],
        compiler_params=params(48),
        cost_estimate=cost(20 * length * length * D, 14 * length * D, length * length * 8),
        name="attend_backward",
    )(packed, packed, packed, grad, logsum, seg_column, seg_row)


def route_kernel(
    hidden_ref,
    attended_ref,
    upstream_ref,
    extra_ref,
    routes_ref,
    targets_ref,
    gain_ref,
    weight_ref,
    small_ref,
    middle_ref,
    normed_ref,
    table_ref,
    rows_ref,
    grads_ref,
    normed_all,
    first_all,
    second_all,
    *,
    token_steps,
    experts,
    constant_count,
    slot_block,
):
    step = pl.program_id(0)
    block = hidden_ref.shape[0]
    kinds = extra_ref.shape[1]

    @pl.when(step < token_steps)
    def _():
        middle = hidden_ref[...].astype(F32) + dot(attended_ref[...], weight_ref[...])
        scale = row_scale(middle)
        normed = (middle * scale * gain_ref[...]).astype(BF16)
        middle_ref[...] = middle
        normed_ref[...] = normed
        upstream = upstream_ref[...]
        wide = upstream.astype(F32)
        small = dot(normed, small_ref[...])
        meets = dot(upstream, small_ref[...])
        inner = jnp.sum(wide * normed.astype(F32), axis=1, keepdims=True)
        logits = small[:, :kinds] + extra_ref[...]
        powers = jnp.exp(logits - jnp.max(logits, axis=1, keepdims=True))
        probs = powers / jnp.sum(powers, axis=1, keepdims=True)
        places = iota((block, kinds), 1)
        table_ref[...] = jnp.zeros_like(table_ref)
        table_ref[:, PROBS : PROBS + kinds] = probs
        table_ref[:, SCALE : SCALE + 1] = scale
        shares = []
        for which in range(constant_count):
            left = small[:, kinds + 2 * which : kinds + 2 * which + 1]
            right = small[:, kinds + 2 * which + 1 : kinds + 2 * which + 2]
            top = jnp.maximum(left, right)
            left, right = jnp.exp(left - top), jnp.exp(right - top)
            both = left + right
            shares.append((left / both, right / both))
        coef = jnp.zeros((block, 1), F32)
        betas = [jnp.zeros((block, 1), F32)] * constant_count
        amounts = [jnp.zeros((block, 1), F32)] * constant_count
        start = kinds + 2 * constant_count
        met = [meets[:, start + which : start + which + 1] for which in range(constant_count)]
        for route in range(2):
            kind = routes_ref[:, route : route + 1]
            chosen = jnp.sum(jnp.where(places == kind, probs, 0.0), axis=1, keepdims=True)
            table_ref[:, CHOSEN + route : CHOSEN + route + 1] = chosen
            part = jnp.where(kind == experts + 1, 1.0, 0.0)
            rest = jnp.zeros((block, 1), F32)
            for which in range(constant_count):
                here = kind == experts + 2 + which
                part = part + jnp.where(here, shares[which][0], 0.0)
                rest = rest + jnp.where(here, shares[which][1] * met[which], 0.0)
                betas[which] = betas[which] + jnp.where(here, chosen * shares[which][1], 0.0)
                amounts[which] = amounts[which] + jnp.where(here, chosen, 0.0)
            coef = coef + chosen * part
            table_ref[:, REST + route : REST + route + 1] = rest + part * inner
            grads = (chosen * wide).astype(BF16)
            rows = pl.ds(pl.multiple_of(step * block, block), block)
            (first_all if route == 0 else second_all)[rows, :] = grads
        normed_all[pl.ds(pl.multiple_of(step * block, block), block), :] = normed
        table_ref[:, COEF : COEF + 1] = coef
        for which in range(constant_count):
            table_ref[:, BETA + which : BETA + which + 1] = betas[which]
            grad_left = amounts[which] * inner
            grad_right = amounts[which] * met[which]
            mean = shares[which][0] * grad_left + shares[which][1] * grad_right
            place = GATE_GRAD + 2 * which
            table_ref[:, place : place + 1] = shares[which][0] * (grad_left - mean)
            table_ref[:, place + 1 : place + 2] = shares[which][1] * (grad_right - mean)

    @pl.when(step >= token_steps)
    def _():
        tokens = normed_all.shape[0]
        slots = (step - token_steps) * slot_block + iota((slot_block, tokens), 0)
        first = jnp.where(slots == targets_ref[0:1, :], 1.0, 0.0)
        second = jnp.where(slots == targets_ref[1:2, :], 1.0, 0.0)
        rows_ref[...] = dot((first + second).astype(BF16), normed_all[...]).astype(BF16)
        grads_ref[...] = (
            dot(first.astype(BF16), first_all[...]) + dot(second.astype(BF16), second_all[...])
        ).astype(BF16)


def route_tokens(
    hidden, attended, upstream, extra, routes, targets, gain, gathered, experts, constant_count, slots
):
    tokens = hidden.shape[0]
    kinds = extra.shape[1]
    steps = tokens // BLOCK
    slot_block = slots // 4
    token_block = lambda width: pl.BlockSpec(
        (BLOCK, width), lambda step: (jnp.minimum(step, steps - 1), 0)
    )
    slot_rows = pl.BlockSpec((slot_block, D), lambda step: (jnp.maximum(step - steps, 0), 0))
    kernel = functools.partial(
        route_kernel,
        token_steps=steps,
        experts=experts,
        constant_count=constant_count,
        slot_block=slot_block,
    )
    return pl.pallas_call(
        kernel,
        grid=(steps + 4,),
        in_specs=[
            token_block(D),
            token_block(D),
            token_block(D),
            token_block(kinds),
            token_block(2),
            whole((2, tokens)),
            whole((1, D)),
            pl.BlockSpec((D, D), lambda step: (0, 3)),
            pl.BlockSpec((D, LANES), lambda step: (0, 4 * D // LANES)),
        ],
        out_specs=[
            token_block(D),
            token_block(D),
            token_block(LANES),
            slot_rows,
            slot_rows,
        ],
        out_shape=[
            jax.ShapeDtypeStruct((tokens, D), F32),
            jax.ShapeDtypeStruct((tokens, D), BF16),
            jax.ShapeDtypeStruct((tokens, LANES), F32),
            jax.ShapeDtypeStruct((slots, D), BF16),
            jax.ShapeDtypeStruct((slots, D), BF16),
        ],
        scratch_shapes=[pltpu.VMEM((tokens, D), BF16)] * 3,
        compiler_params=params(40),
        cost_estimate=cost(2 * tokens * D * (D + 3 * slots), 20 * tokens * D),
        name="route_tokens",
    )(hidden, attended, upstream, extra, routes, targets, gain, gathered, gathered)


def expert_kernel(
    rows_ref, grads_ref, gate_ref, up_ref, outer_ref, active_ref, grad_gate_ref, grad_up_ref, produced_ref, total
):
    step = pl.program_id(0)
    gate = dot(rows_ref[...], gate_ref[...])
    up = dot(rows_ref[...], up_ref[...])
    sigmoid = 1.0 / (1.0 + jnp.exp(-gate))
    silu = gate * sigmoid
    active = (silu * up).astype(BF16)
    active_ref[...] = active
    part = dot(active, outer_ref[...])
    total[...] = jnp.where(step == 0, part, total[...] + part)
    grad_active = dot(grads_ref[...], outer_ref[...], NT)
    grad_gate_ref[...] = (grad_active * up * sigmoid * (1.0 + gate * (1.0 - sigmoid))).astype(BF16)
    grad_up_ref[...] = (grad_active * silu).astype(BF16)

    @pl.when(step == pl.num_programs(0) - 1)
    def _():
        produced_ref[...] = total[...].astype(BF16)


def expert_forward(rows, grads, inner, outer):
    count = rows.shape[0]
    steps = FF // BLOCK
    hidden_block = pl.BlockSpec((count, BLOCK), lambda step: (0, step))
    return pl.pallas_call(
        expert_kernel,
        grid=(steps,),
        in_specs=[
            whole((count, D)),
            whole((count, D)),
            pl.BlockSpec((D, BLOCK), lambda step: (0, step)),
            pl.BlockSpec((D, BLOCK), lambda step: (0, steps + step)),
            pl.BlockSpec((BLOCK, D), lambda step: (step, 0)),
        ],
        out_specs=[hidden_block, hidden_block, hidden_block, whole((count, D))],
        out_shape=[jax.ShapeDtypeStruct((count, FF), BF16)] * 3
        + [jax.ShapeDtypeStruct((count, D), BF16)],
        scratch_shapes=[pltpu.VMEM((count, D), F32)],
        compiler_params=params(48),
        cost_estimate=cost(8 * count * D * FF, 6 * count * FF + 6 * D * FF, count * FF),
        name="expert_forward",
    )(rows, grads, inner, inner, outer)


def mix_kernel(
    returned_ref,
    targets_ref,
    routes_ref,
    table_ref,
    middle_ref,
    normed_ref,
    upstream_ref,
    small_ref,
    out_ref,
    grads_ref,
    logits_ref,
    work,
    *,
    kinds,
    constant_count,
):
    block = middle_ref.shape[0]
    slots = returned_ref.shape[0]
    wide = upstream_ref[...].astype(F32)
    table = table_ref[...]
    probs = table[:, PROBS : PROBS + kinds]
    places = iota((block, kinds), 1)
    columns = iota((block, slots), 1)
    blended = normed_ref[...].astype(F32) * table[:, COEF : COEF + 1]
    grad_probs = jnp.zeros((block, kinds), F32)
    for route in range(2):
        hot = jnp.where(columns == targets_ref[:, route : route + 1], 1.0, 0.0).astype(BF16)
        paired = dot(hot, returned_ref[...])
        blended = blended + table[:, CHOSEN + route : CHOSEN + route + 1] * paired
        grad_chosen = (
            jnp.sum(wide * paired, axis=1, keepdims=True) + table[:, REST + route : REST + route + 1]
        )
        grad_probs = grad_probs + jnp.where(
            places == routes_ref[:, route : route + 1], grad_chosen, 0.0
        )
    grad_logits = probs * (grad_probs - jnp.sum(probs * grad_probs, axis=1, keepdims=True))
    logits_ref[...] = grad_logits
    gates = 2 * constant_count
    work[...] = jnp.zeros_like(work)
    work[:, :kinds] = grad_logits
    work[:, kinds : kinds + gates] = table[:, GATE_GRAD : GATE_GRAD + gates]
    work[:, kinds + gates : kinds + gates + constant_count] = table[:, BETA : BETA + constant_count]
    values = work[...]
    upper = values.astype(BF16)
    lower = (values - upper.astype(F32)).astype(BF16)
    grads_ref[:, :LANES] = upper
    grads_ref[:, LANES:] = lower
    is_value = iota((block, LANES), 1) >= kinds + gates
    nothing = jnp.zeros((block, LANES), BF16)
    blended = blended + (
        dot(jnp.where(is_value, upper, nothing), small_ref[...], NT)
        + dot(jnp.where(is_value, lower, nothing), small_ref[...], NT)
    )
    out_ref[...] = (middle_ref[...] + blended).astype(BF16)


def mix_branches(
    returned, targets, routes, table, middle, normed, upstream, gathered, kinds, constant_count
):
    tokens = middle.shape[0]
    slots = returned.shape[0]
    token_block = lambda width: pl.BlockSpec((BLOCK, width), lambda step: (step, 0))
    return pl.pallas_call(
        functools.partial(mix_kernel, kinds=kinds, constant_count=constant_count),
        grid=(tokens // BLOCK,),
        in_specs=[
            whole((slots, D)),
            token_block(2),
            token_block(2),
            token_block(LANES),
            token_block(D),
            token_block(D),
            token_block(D),
            pl.BlockSpec((D, LANES), lambda step: (0, 4 * D // LANES)),
        ],
        out_specs=[token_block(D), token_block(2 * LANES), token_block(kinds)],
        out_shape=[
            jax.ShapeDtypeStruct((tokens, D), BF16),
            jax.ShapeDtypeStruct((tokens, 2 * LANES), BF16),
            jax.ShapeDtypeStruct((tokens, kinds), F32),
        ],
        scratch_shapes=[pltpu.VMEM((BLOCK, LANES), F32)],
        compiler_params=params(40),
        cost_estimate=cost(4 * tokens * D * slots, 14 * tokens * D),
        name="mix_branches",
    )(returned, targets, routes, table, middle, normed, upstream, gathered)


def middle_kernel(
    returned_ref,
    targets_ref,
    table_ref,
    grads_ref,
    middle_ref,
    upstream_ref,
    small_ref,
    gain_ref,
    weight_ref,
    grad_middle_ref,
    rounded_ref,
    attended_ref,
    grad_gain_ref,
    *,
    gate_end,
):
    block = middle_ref.shape[0]
    slots = returned_ref.shape[0]
    columns = iota((block, slots), 1)
    hot = jnp.where(columns == targets_ref[:, 0:1], 1.0, 0.0) + jnp.where(
        columns == targets_ref[:, 1:2], 1.0, 0.0
    )
    total = dot(hot.astype(BF16), returned_ref[...])
    wide = upstream_ref[...].astype(F32)
    total = total + wide * table_ref[:, COEF : COEF + 1]
    is_small = iota((block, LANES), 1) < gate_end
    nothing = jnp.zeros((block, LANES), BF16)
    total = total + (
        dot(jnp.where(is_small, grads_ref[:, :LANES], nothing), small_ref[...], NT)
        + dot(jnp.where(is_small, grads_ref[:, LANES:], nothing), small_ref[...], NT)
    )
    scale = table_ref[:, SCALE : SCALE + 1]
    unit = middle_ref[...] * scale
    part = jnp.sum(total * unit, axis=0, keepdims=True)
    grad_gain_ref[...] = jnp.where(pl.program_id(0) == 0, part, grad_gain_ref[...] + part)
    inner = total * gain_ref[...]
    grad_middle = wide + scale * (inner - unit * jnp.mean(inner * unit, axis=1, keepdims=True))
    grad_middle_ref[...] = grad_middle
    rounded = grad_middle.astype(BF16)
    rounded_ref[...] = rounded
    attended_ref[...] = dot(rounded, weight_ref[...], NT).astype(BF16)


def middle_backward(returned, targets, table, grads, middle, upstream, gain, gathered, gate_end):
    tokens = middle.shape[0]
    slots = returned.shape[0]
    token_block = lambda width: pl.BlockSpec((BLOCK, width), lambda step: (step, 0))
    return pl.pallas_call(
        functools.partial(middle_kernel, gate_end=gate_end),
        grid=(tokens // BLOCK,),
        in_specs=[
            whole((slots, D)),
            token_block(2),
            token_block(LANES),
            token_block(2 * LANES),
            token_block(D),
            token_block(D),
            pl.BlockSpec((D, LANES), lambda step: (0, 4 * D // LANES)),
            whole((1, D)),
            pl.BlockSpec((D, D), lambda step: (0, 3)),
        ],
        out_specs=[token_block(D), token_block(D), token_block(D), whole((1, D))],
        out_shape=[
            jax.ShapeDtypeStruct((tokens, D), F32),
            jax.ShapeDtypeStruct((tokens, D), BF16),
            jax.ShapeDtypeStruct((tokens, D), BF16),
            jax.ShapeDtypeStruct((1, D), F32),
        ],
        compiler_params=params(40),
        cost_estimate=cost(2 * tokens * D * (slots + D), 18 * tokens * D),
        name="middle_backward",
    )(returned, targets, table, grads, middle, upstream, gathered, gain, gathered)


def input_kernel(packed_ref, weight_ref, hidden_ref, grad_middle_ref, gain_ref, out_ref, grad_gain_ref):
    total = dot(packed_ref[...], weight_ref[...], NT)
    values = hidden_ref[...].astype(F32)
    scale = row_scale(values)
    unit = values * scale
    part = jnp.sum(total * unit, axis=0, keepdims=True)
    grad_gain_ref[...] = jnp.where(pl.program_id(0) == 0, part, grad_gain_ref[...] + part)
    inner = total * gain_ref[...]
    out_ref[...] = grad_middle_ref[...] + scale * (
        inner - unit * jnp.mean(inner * unit, axis=1, keepdims=True)
    )


def input_backward(grad_packed, gathered, hidden, grad_middle, gain):
    tokens = hidden.shape[0]
    token_block = lambda width: pl.BlockSpec((BLOCK, width), lambda step: (step, 0))
    return pl.pallas_call(
        input_kernel,
        grid=(tokens // BLOCK,),
        in_specs=[
            token_block(3 * D),
            pl.BlockSpec((D, 3 * D), lambda step: (0, 0)),
            token_block(D),
            token_block(D),
            whole((1, D)),
        ],
        out_specs=[token_block(D), whole((1, D))],
        out_shape=[
            jax.ShapeDtypeStruct((tokens, D), F32),
            jax.ShapeDtypeStruct((1, D), F32),
        ],
        compiler_params=params(40),
        cost_estimate=cost(6 * tokens * D * D, 16 * tokens * D),
        name="input_backward",
    )(grad_packed, gathered, hidden, grad_middle, gain)


def pair_targets(routes, priority, experts, total_kinds, capacity):
    kind_ids = jnp.arange(total_kinds, dtype=jnp.int32)
    hot = [(routes[:, k : k + 1] == kind_ids[None, :]).astype(F32) for k in range(2)]
    earlier = (priority[None, :] < priority[:, None]).astype(BF16)
    before = dot(earlier, (hot[0] + hot[1]).astype(BF16))
    slots = jnp.stack([jnp.sum(before * one, axis=1) for one in hot], axis=1).astype(jnp.int32)
    kept_pairs = jnp.logical_and(routes < experts, slots < capacity)
    return jnp.where(kept_pairs, routes * capacity + slots, experts * capacity)


def exchange(blocks, axis):
    return lax.all_to_all(blocks, axis, split_axis=0, concat_axis=0, tiled=True)


def adam_step(master, first, second, grad, factor, step_rate):
    clipped = grad * factor
    first_new = beta_moment * first + (1.0 - beta_moment) * clipped
    second_new = beta_moment * second + (1.0 - beta_moment) * clipped * clipped
    correct = 1.0 - beta_moment**step_number
    update = (
        first_new / correct / (jnp.sqrt(second_new / correct) + adam_epsilon) + decay_rate * master
    )
    master_new = master - step_rate * update
    return (grad, master_new, first_new, second_new, master_new.astype(jnp.bfloat16))


def body(
    hidden_in,
    gate_prior,
    routes,
    priority,
    segments,
    cotangent,
    attend_in,
    first_attend_in,
    second_attend_in,
    attend_out,
    first_attend_out,
    second_attend_out,
    router,
    first_router,
    second_router,
    gate_mix,
    first_gate_mix,
    second_gate_mix,
    constants,
    first_constants,
    second_constants,
    norm_gains,
    first_norm_gains,
    second_norm_gains,
    expert_in,
    first_expert_in,
    second_expert_in,
    expert_out,
    first_expert_out,
    second_expert_out,
):
    groups = lax.axis_size("expert")
    devices = lax.axis_size("dp") * groups
    kinds = gate_prior.shape[1]
    constant_count = constants.shape[1] // 3
    experts = kinds - 2 - constant_count
    token_count = hidden_in.shape[0]
    width_top = routes.shape[1]
    capacity = max(2, width_top * token_count // kinds // 8 * 8)
    slots = experts * capacity
    small_width = kinds + 3 * constant_count
    gate_end = kinds + 2 * constant_count

    mine = jnp.concatenate(
        [
            attend_in,
            attend_out,
            router,
            constants,
            norm_gains.T,
            jnp.zeros((attend_in.shape[0], LANES - small_width - 2), F32),
        ],
        axis=1,
    ).astype(BF16)
    gathered = lax.all_gather(mine, BOTH, axis=0, tiled=True)
    expert_inner = lax.all_gather(expert_in.astype(BF16), "dp", axis=1, tiled=True)[0]
    expert_outer = lax.all_gather(expert_out.astype(BF16), "dp", axis=1, tiled=True)[0]
    gains = gathered[:, 4 * D + small_width : 4 * D + small_width + 2].astype(F32).T
    gain_first, gain_second = gains[0:1], gains[1:2]

    targets = pair_targets(routes, priority[0], experts, kinds, capacity)
    target_rows = targets.T
    extra = jnp.dot(gate_prior, gate_mix.astype(BF16).astype(F32), precision=highest)
    seg_row = segments
    seg_column = segments.reshape(token_count, 1)

    normed_first, packed = project(hidden_in, gain_first, gathered)
    attended, logsum = attend_forward(packed, seg_column, seg_row)
    logsum = jnp.transpose(logsum, (0, 2, 1))
    middle, normed_second, table, rows, row_grads = route_tokens(
        hidden_in,
        attended,
        cotangent,
        extra,
        routes,
        target_rows,
        gain_second,
        gathered,
        experts,
        constant_count,
        slots,
    )
    split = (groups, slots // groups, D)
    arrived = exchange(rows.reshape(split), "expert").reshape(slots, D)
    arrived_grad = exchange(row_grads.reshape(split), "expert").reshape(slots, D)
    active, grad_gate, grad_up, produced = expert_forward(
        arrived, arrived_grad, expert_inner, expert_outer
    )
    returned = exchange(produced.reshape(split), "expert").reshape(slots, D)
    grad_joined = jnp.concatenate([grad_gate, grad_up], axis=1)
    grad_rows = dot(grad_joined, expert_inner, NT).astype(BF16)
    grad_returned = exchange(grad_rows.reshape(split), "expert").reshape(slots, D)
    grad_outer = dot(active, arrived_grad, TN).astype(BF16)
    grad_inner = dot(arrived, grad_joined, TN).astype(BF16)
    grad_outer_own = lax.psum_scatter(grad_outer[None], "dp", scatter_dimension=1, tiled=True)
    grad_inner_own = lax.psum_scatter(grad_inner[None], "dp", scatter_dimension=1, tiled=True)

    activations, token_grads, grad_logits = mix_branches(
        returned,
        targets,
        routes,
        table,
        middle,
        normed_second,
        cotangent,
        gathered,
        kinds,
        constant_count,
    )
    grad_middle, rounded, grad_attended, grad_gain_second = middle_backward(
        grad_returned, targets, table, token_grads, middle, cotangent, gain_second, gathered, gate_end
    )
    from_normed = dot(normed_second, token_grads, TN)
    from_upstream = dot(cotangent, token_grads, TN)
    column = jnp.arange(LANES)[None, :]
    grad_small = jnp.where(
        column < gate_end,
        from_normed[:, :LANES] + from_normed[:, LANES:],
        from_upstream[:, :LANES] + from_upstream[:, LANES:],
    )
    grad_mixer = jnp.einsum("tk,tj->kj", gate_prior, grad_logits, precision=highest)
    grad_out_and_small = jnp.concatenate(
        [dot(attended, rounded, TN).astype(BF16), grad_small.astype(BF16)], axis=1
    )
    out_own = lax.psum_scatter(grad_out_and_small, BOTH, scatter_dimension=0, tiled=True).astype(F32)

    grad_packed = attend_backward(packed, grad_attended, logsum, seg_column, seg_row)
    grad_weight_in = dot(normed_first, grad_packed, TN).astype(BF16)
    in_own = lax.psum_scatter(grad_weight_in, BOTH, scatter_dimension=0, tiled=True).astype(F32)
    input_grad, grad_gain_first = input_backward(
        grad_packed, gathered, hidden_in, grad_middle, gain_first
    )

    width = norm_gains.shape[1]
    grad_gains = jnp.concatenate([grad_gain_first, grad_gain_second], axis=0)
    for_each = grad_gains.reshape(2, devices, width).transpose(1, 0, 2).reshape(devices, 2 * width)
    mixer_flat = jnp.broadcast_to(grad_mixer.reshape(1, kinds * kinds), (devices, kinds * kinds))
    few = jnp.concatenate([for_each, mixer_flat], axis=1)
    few = exchange(few[:, None, :], BOTH).sum(axis=(0, 1))
    gains_own = few[: 2 * width].reshape(2, width)
    mixer_total = few[2 * width :].reshape(kinds, kinds)

    dense_own = (
        in_own,
        out_own[:, :D],
        out_own[:, D : D + kinds],
        out_own[:, D + kinds : D + small_width],
        gains_own,
    )
    owned_grads = dense_own + (grad_inner_own.astype(F32), grad_outer_own.astype(F32))
    partial_square = sum((jnp.sum(member * member) for member in owned_grads))
    squares = exchange(jnp.broadcast_to(partial_square, (devices, 1, LANES)), BOTH)
    square_total = jnp.sum(squares[:, 0, 0])
    grad_norm = jnp.sqrt(square_total + jnp.sum(mixer_total * mixer_total))
    factor = clip_limit / jnp.maximum(grad_norm, clip_limit)
    results = (activations, input_grad, grad_norm)
    states = (
        (attend_in, first_attend_in, second_attend_in, owned_grads[0]),
        (attend_out, first_attend_out, second_attend_out, owned_grads[1]),
        (router, first_router, second_router, owned_grads[2]),
        (gate_mix, first_gate_mix, second_gate_mix, mixer_total),
        (constants, first_constants, second_constants, owned_grads[3]),
        (norm_gains, first_norm_gains, second_norm_gains, owned_grads[4]),
        (expert_in, first_expert_in, second_expert_in, owned_grads[5]),
        (expert_out, first_expert_out, second_expert_out, owned_grads[6]),
    )
    for state, rate in zip(states, learn_rates):
        results = results + adam_step(*state, factor, rate)
    return results


def solution(mesh):
    in_specs = (
        P(("dp", "expert"), None),
        P(("dp", "expert"), None),
        P(("dp", "expert"), None),
        P(("dp", "expert"), None),
        P(("dp", "expert"), None),
        P(("dp", "expert"), None),
        P(("dp", "expert"), None),
        P(("dp", "expert"), None),
        P(("dp", "expert"), None),
        P(("dp", "expert"), None),
        P(("dp", "expert"), None),
        P(("dp", "expert"), None),
        P(("dp", "expert"), None),
        P(("dp", "expert"), None),
        P(("dp", "expert"), None),
        P(),
        P(),
        P(),
        P(("dp", "expert"), None),
        P(("dp", "expert"), None),
        P(("dp", "expert"), None),
        P(None, ("dp", "expert")),
        P(None, ("dp", "expert")),
        P(None, ("dp", "expert")),
        P("expert", "dp", None),
        P("expert", "dp", None),
        P("expert", "dp", None),
        P("expert", "dp", None),
        P("expert", "dp", None),
        P("expert", "dp", None),
    )
    out_specs = (
        P(("dp", "expert"), None),
        P(("dp", "expert"), None),
        P(),
        P(("dp", "expert"), None),
        P(("dp", "expert"), None),
        P(("dp", "expert"), None),
        P(("dp", "expert"), None),
        P(("dp", "expert"), None),
        P(("dp", "expert"), None),
        P(("dp", "expert"), None),
        P(("dp", "expert"), None),
        P(("dp", "expert"), None),
        P(("dp", "expert"), None),
        P(("dp", "expert"), None),
        P(("dp", "expert"), None),
        P(("dp", "expert"), None),
        P(("dp", "expert"), None),
        P(("dp", "expert"), None),
        P(),
        P(),
        P(),
        P(),
        P(),
        P(("dp", "expert"), None),
        P(("dp", "expert"), None),
        P(("dp", "expert"), None),
        P(("dp", "expert"), None),
        P(("dp", "expert"), None),
        P(None, ("dp", "expert")),
        P(None, ("dp", "expert")),
        P(None, ("dp", "expert")),
        P(None, ("dp", "expert")),
        P(None, ("dp", "expert")),
        P("expert", "dp", None),
        P("expert", "dp", None),
        P("expert", "dp", None),
        P("expert", "dp", None),
        P("expert", "dp", None),
        P("expert", "dp", None),
        P("expert", "dp", None),
        P("expert", "dp", None),
        P("expert", "dp", None),
        P("expert", "dp", None),
    )
    return jax.shard_map(body, mesh=mesh, in_specs=in_specs, out_specs=out_specs, check_vma=False)
```

time: 1200 us -> 818 us (0.68)
  matrix products: 334 us -> 43.3 us
  blocking collectives: 198 us -> 23.3 us
  Pallas kernels: 0 us -> 148 us
  waiting for transfers between devices: 364 us -> 462 us
  local copies, waits for them, and re-layouts: 146 us -> 59.7 us
  other arithmetic: 112 us -> 34.3 us
    dot_general x27 -> x10, matrix products: 334 us -> 43.3 us  [the longest x8 39.8 us: dot(): return lax.dot_general(left, right, form, preferred_element_type=F32)]
    pallas_call x0 -> x8, Pallas kernels: none -> 148 us  [the longest x1 45.2 us: attend_backward(): pl.pallas_call(functools.partial(attend_backward_kernel, block=2 * BLOCK)...]
    all_gather x3 -> x0, blocking collectives: 119 us -> none  [the longest x1 43.1 us: body(): lax.all_gather(norm_gains.astype(jnp.bfloat16), ('dp', 'expert'), axis=1,...]
    all_gather x4 -> x3, waiting for transfers between devices: 0.06 us -> 108 us  [the longest x1 59.1 us: body(): gathered = lax.all_gather(mine, BOTH, axis=0, tiled=True)]
    gather x17 -> x0, local copies, waits for them, and re-layouts: 79.4 us -> none  [the longest x3 25.7 us: body(): jnp.take(returned.reshape(experts * capacity, D), targets, axis=0, mode='...]
    reduce_scatter x4 -> x3, waiting for transfers between devices: 348 us -> 295 us  [the longest x1 119 us: body(): lax.psum_scatter(grad_inner[None], 'dp', scatter_dimension=1, tiled=True)]
    reduce_sum x9 -> x2, other arithmetic: 43.4 us -> 0.68 us  [the longest x1 0.63 us: body(): square_total = jnp.sum(squares[:, 0, 0])]
    unnamed x1 -> x0, blocking collectives: 39.7 us -> none
  transfers between devices with their start and end apart: 12 -> 12, of which waited for: 5 -> 10; matrix products, arithmetic and copies ran while one was open for 39% -> 9% of each run, Pallas kernels for 0% -> 14%
where the time goes in v1:
time: 818 us; the launch traced here: 813 us
  waiting for transfers between devices  462 us (56%)
  Pallas kernels  148 us (18%)
  local copies, waits for them, and re-layouts  59.7 us (7%)
  matrix products  43.3 us (5%)
  other arithmetic  34.3 us (4%)
  blocking collectives  23.3 us (3%)
  between operations  22.3 us (3%)
  starting transfers between devices  20.8 us (3%)
    reduce_scatter x1, waiting for transfers between devices, body(): lax.psum_scatter(grad_inner[None], 'dp', scatter_dimension=1, tiled=True)  119 us
    reduce_scatter x1, waiting for transfers between devices, body(): lax.psum_scatter(grad_weight_in, BOTH, scatter_dimension=0, tiled=True)  104 us
    reduce_scatter x1, waiting for transfers between devices, body(): lax.psum_scatter(grad_outer[None], 'dp', scatter_dimension=1, tiled=True)  71.6 us
    all_gather x1, waiting for transfers between devices, body(): gathered = lax.all_gather(mine, BOTH, axis=0, tiled=True)  59.1 us
    unnamed x154, local copies, waits for them, and re-layouts  51.3 us
    all_gather x1, waiting for transfers between devices, body(): lax.all_gather(expert_in.astype(BF16), 'dp', axis=1, tiled=True)[0]  48.9 us
    pallas_call x1, Pallas kernels, attend_backward(): pl.pallas_call(functools.partial(attend_backward_kernel, block=2 * BLOCK)...  45.2 us
    dot_general x8, matrix products, dot(): return lax.dot_general(left, right, form, preferred_element_type=F32)  39.8 us
  transfers between devices with their start and end apart: 12, of which 10 were waited for; matrix products, arithmetic and copies ran while one was open for 9% of the time, Pallas kernels for 14%

profile of v1, /device:TPU:0, one launch (start us, length us, event | category | flops | bytes accessed | tf_op | source)
XLA Modules:
  0.0 813.1 jit_solution(2390252484878225364)
XLA Ops:
  20.6 59.1 %all-gather.4.cloned.1.call-done.weight_ref.small_ref = bf16[768,3200]{1,0:T(8,128)(2,1)} async-done(((bf16[24,3200]{1,0:T(8,128)(2,1)}), bf16[768,3200]{1,0:T(8,128)(2,1)}) %all-gather.4.cloned.1.call-update) | async-done | bytes 4915216 | tf_op jit(solution)/shard_map/all_gather | solution.py:721
  80.8 2.4 copy-done.1
  83.2 5.6 project.1
  92.2 24.5 %attend_forward.1 = (bf16[1024,768]{1,0:T(8,128)(2,1)S(1)}, f32[6,1024,2]{2,1,0:T(8,128)S(1)}) custom-call(bf16[1024,2304]{1,0:T(8,128)(2,1)} %copy-done.35, bf16[1024,2304]{1,0:T(8,128)(2,1)} %copy-done.35, bf16[1024,2304]{1,0:T(8,128)(2,1)} %copy-done.35, s32[1024,1]{1,0:T(8,128)S(1)} %copy.230.seg_column_ref, s32[1,1024]{1,0:T(1,128)S(1)} %copy-done.32), custom_call_target="tpu_custom_call" | custom-call | flops 6442450944 | bytes 6291456 | tf_op jit(solution)/shard_map/attend_forward/pallas_call | solution.py:124
  118.4 24.7 %route_tokens.1 = (f32[1024,768]{1,0:T(8,128)S(1)}, bf16[1024,768]{1,0:T(8,128)(2,1)S(1)}, f32[1024,128]{1,0:T(8,128)S(1)}, bf16[1024,768]{1,0:T(8,128)(2,1)S(1)}, bf16[1024,768]{1,0:T(8,128)(2,1)S(1)}) custom-call(bf16[1024,768]{1,0:T(8,128)(2,1)S(1)} %copy-done.26, bf16[1024,768]{1,0:T(8,128)(2,1)S(1)} %get-tuple-element.66.attended_ref, ...), custom_call_target="tpu_custom_call" | custom-call | flops 6039797760 | bytes 15728640 | tf_op jit(solution)/shard_map/route_tokens/pallas_call | solution.py:359
  145.1 23.3 %all_to_all.30 = bf16[4,256,768]{2,1,0:T(8,128)(2,1)} all-to-all(bf16[4,256,768]{2,1,0:T(8,128)(2,1)S(1)} %bitcast.56), channel_id=1, replica_groups=mesh['dp'=8,'expert'=4] {'expert'}, dimensions={0} | all-to-all | bytes 3145728 | tf_op jit(solution)/shard_map/all_to_all | solution.py:651
  168.3 4.8 all-to-all-start
  173.2 20.1 %all-to-all-done = bf16[4,256,768]{2,1,0:T(8,128)(2,1)} async-done(((bf16[4,256,768]{2,1,0:T(8,128)(2,1)}), bf16[4,256,768]{2,1,0:T(8,128)(2,1)}, u32[]{:S(2)}, u32[]{:S(2)}) %all-to-all-start) | async-done | bytes 1572896 | tf_op jit(solution)/shard_map/all_to_all | solution.py:651
  193.3 48.9 %all-gather.6.cloned.1.call-done = bf16[1,768,4096]{2,1,0:T(8,128)(2,1)} async-done(((bf16[1,96,4096]{2,1,0:T(8,128)(2,1)}), bf16[1,768,4096]{2,1,0:T(8,128)(2,1)}) %all-gather.6.cloned.1.call-update) | async-done | bytes 6291472 | tf_op jit(solution)/shard_map/all_gather | solution.py:722
  243.5 21.4 %expert_forward.1 = (bf16[1024,2048]{1,0:T(8,128)(2,1)}, bf16[1024,2048]{1,0:T(8,128)(2,1)}, bf16[1024,2048]{1,0:T(8,128)(2,1)}, bf16[1024,768]{1,0:T(8,128)(2,1)S(1)}) custom-call(bf16[1024,768]{1,0:T(8,128)(2,1)} %bitcast.10.rows_ref, bf16[1024,768]{1,0:T(8,128)(2,1)S(1)} %bitcast.52, bf16[768,4096]{1,0:T(8,128)(2,1)} %bitcast.70, ...), custom_call_target="tpu_custom_call" | custom-call | flops 12884901888 | bytes 22020096 | tf_op jit(solution)/shard_map/expert_forward/pallas_call | solution.py:419
  266.1 4.3 all-to-all-start.2
  270.4 2.7 constant_dynamic-update-slice_fusion.1
  274.2 3.4 copy-done.48
  277.6 7.8 convolution_convert_fusion.3
  285.4 5.2 all-to-all-done.2
  290.6 4.4 all-to-all-start.3
  302.4 10.7 %mix_branches.1 = (bf16[1024,768]{1,0:T(8,128)(2,1)}, bf16[1024,256]{1,0:T(8,128)(2,1)S(1)}, f32[1024,8]{1,0:T(8,128)S(1)}) custom-call(bf16[1024,768]{1,0:T(8,128)(2,1)} %bitcast.16.returned_ref, s32[1024,2]{1,0:T(8,128)S(1)} %copy-done.8, s32[1024,2]{1,0:T(8,128)S(1)} %copy-done.20, f32[1024,128]{1,0:T(8,128)S(1)} %copy-done.17, ...), custom_call_target="tpu_custom_call" | custom-call | flops 3221225472 | bytes 11010048 | tf_op jit(solution)/shard_map/mix_branches/pallas_call | solution.py:502
  319.1 8.9 %middle_backward.1 = (f32[1024,768]{1,0:T(8,128)S(1)}, bf16[1024,768]{1,0:T(8,128)(2,1)S(1)}, bf16[1024,768]{1,0:T(8,128)(2,1)S(1)}, f32[1,768]{1,0:T(1,128)S(1)}) custom-call(bf16[1024,768]{1,0:T(8,128)(2,1)} %bitcast.18.returned_ref, s32[1024,2]{1,0:T(8,128)S(1)} %copy-done.9, f32[1024,128]{1,0:T(8,128)S(1)} %copy-done.18, ...), custom_call_target="tpu_custom_call" | custom-call | flops 2818572288 | bytes 14155776 | tf_op jit(solution)/shard_map/middle_backward/pallas_call | solution.py:576
  332.8 45.2 %attend_backward.1.packed_ref = bf16[1024,2304]{1,0:T(8,128)(2,1)} custom-call(bf16[1024,2304]{1,0:T(8,128)(2,1)} %copy-done.35, bf16[1024,2304]{1,0:T(8,128)(2,1)} %copy-done.35, bf16[1024,2304]{1,0:T(8,128)(2,1)} %copy-done.35, bf16[1024,768]{1,0:T(8,128)(2,1)S(1)} %copy-done.34, f32[6,2,1024]{2,1,0:T(2,128)S(1)} %bitcast.57, s32[1024,1]{1,0:T(8,128)S(1)} %copy-done.29, ...), custom_call_target="tpu_custom_call" | custom-call | flops 16106127360 | bytes 11010048 | tf_op jit(solution)/shard_map/attend_backward/pallas_call | solution.py:214
  378.0 7.6 convolution_convert_fusion.1
  387.1 7.5 fusion.3
  394.6 11.6 %fusion = bf16[1,768,4096]{2,1,0:T(8,128)(2,1)} fusion(bf16[1024,768]{1,0:T(8,128)(2,1)} %bitcast.10.rows_ref, bf16[1024,4096]{1,0:T(8,128)(2,1)} %copy-done.48), kind=kOutput, calls=%fused_computation.1 | convolution fusion | flops 6445596672 | bytes 16252928 | tf_op jit(solution)/shard_map/dot_general | solution.py:39
  408.6 2.4 copy-done.2
  414.8 6.4 input_backward.1
  422.2 3.2 all-to-all-start.4
  429.5 3.0 all-to-all-done.4
  433.2 28.6 %all-reduce.3.cloned.1.call-done = bf16[768,896]{0,1:T(8,128)(2,1)} async-done(((bf16[768,896]{0,1:T(8,128)(2,1)}), bf16[768,896]{0,1:T(8,128)(2,1)}) %all-reduce.3.cloned.1.call-update) | async-done | bytes 1376272
  465.6 104.2 %reduce-scatter.5.cloned.1.call-done = bf16[24,2304]{1,0:T(8,128)(2,1)} async-done(((bf16[768,2304]{1,0:T(8,128)(2,1)}), bf16[24,2304]{1,0:T(8,128)(2,1)}) %reduce-scatter.5.cloned.1.call-update) | async-done | bytes 110608 | tf_op jit(solution)/shard_map/reduce_scatter | solution.py:795
  575.2 71.6 %reduce-scatter.9.cloned.1.call-done = bf16[1,256,768]{2,1,0:T(8,128)(2,1)} async-done(((bf16[1,2048,768]{2,1,0:T(8,128)(2,1)}), bf16[1,256,768]{2,1,0:T(8,128)(2,1)}) %reduce-scatter.9.cloned.1.call-update) | async-done | bytes 393232 | tf_op jit(solution)/shard_map/reduce_scatter | solution.py:761
  648.7 118.9 %reduce-scatter.7.cloned.1.call-done = bf16[1,96,4096]{2,1,0:T(8,128)(2,1)} async-done(((bf16[1,768,4096]{2,1,0:T(8,128)(2,1)}), bf16[1,96,4096]{2,1,0:T(8,128)(2,1)}) %reduce-scatter.7.cloned.1.call-update) | async-done | bytes 786448 | tf_op jit(solution)/shard_map/reduce_scatter | solution.py:762
  771.8 3.8 all-to-all-start.5
  801.6 3.4 fusion.23
  (237 shorter events, 91.3 us)
Async XLA Ops:
  7.2 11.9 %copy-start = (f32[1024,8]{0,1:T(8,128)S(1)}, f32[1024,8]{0,1:T(8,128)}, u32[]{:S(2)}) copy-start(f32[1024,8]{0,1:T(8,128)} %param.31) | copy-start | bytes 98308
  7.3 72.4 %all-gather.4.cloned.1.call-start = ((), (), s32[]{:S(2)}) async-start(), calls=%async_computation.9 | async-start | bytes 5068800 | tf_op jit(solution)/shard_map/all_gather | solution.py:721
  12.4 160.8 %all-gather.8.cloned.1.call-start = ((), (), s32[]{:S(2)}) async-start(), calls=%async_computation.11 | async-start | bytes 3538944 | tf_op jit(solution)/shard_map/all_gather | solution.py:723
  14.4 227.7 %all-gather.6.cloned.1.call-start = ((), (), s32[]{:S(2)}) async-start(), calls=%async_computation.10 | async-start | bytes 7077888 | tf_op jit(solution)/shard_map/all_gather | solution.py:722
  18.6 70.2 %copy-start.7 = (s32[1024,2]{1,0:T(8,128)}, s32[1024,2]{1,0:T(8,128)S(1)}, u32[]{:S(2)}) copy-start(s32[1024,2]{1,0:T(8,128)S(1)} %add_select_fusion.targets_ref) | copy-start | bytes 24580
  18.6 62.2 %copy-start.25 = (bf16[1024,768]{1,0:T(8,128)(2,1)S(1)}, bf16[1024,768]{1,0:T(8,128)(2,1)}, u32[]{:S(2)}) copy-start(bf16[1024,768]{1,0:T(8,128)(2,1)} %hidden_ref.5) | copy-start | bytes 4718596
  19.2 73.0 %copy-start.28 = (s32[1024,1]{1,0:T(8,128)}, s32[1024,1]{1,0:T(8,128)S(1)}, u32[]{:S(2)}) copy-start(s32[1024,1]{1,0:T(8,128)S(1)} %copy.230.seg_column_ref) | copy-start | bytes 12292
  92.1 26.2 %copy-start.3 = (bf16[1024,768]{1,0:T(8,128)(2,1)S(1)}, bf16[1024,768]{1,0:T(8,128)(2,1)}, u32[]{:S(2)}) copy-start(bf16[1024,768]{1,0:T(8,128)(2,1)} %upstream_ref.5) | copy-start | bytes 4718596
  92.1 26.2 %copy-start.19 = (s32[1024,2]{1,0:T(8,128)S(1)}, s32[1024,2]{1,0:T(8,128)}, u32[]{:S(2)}) copy-start(s32[1024,2]{1,0:T(8,128)} %copy.236.routes_ref) | copy-start | bytes 24580
  92.1 26.2 %copy-start.26 = (bf16[1024,768]{1,0:T(8,128)(2,1)S(1)}, bf16[1024,768]{1,0:T(8,128)(2,1)}, u32[]{:S(2)}) copy-start(bf16[1024,768]{1,0:T(8,128)(2,1)} %hidden_ref.5) | copy-start | bytes 4718596
  92.1 26.2 %copy-start.31 = (f32[1024,8]{1,0:T(8,128)S(1)}, f32[1024,8]{1,0:T(8,128)}, u32[]{:S(2)}) copy-start(f32[1024,8]{1,0:T(8,128)} %fusion.17.extra_ref) | copy-start | bytes 98308
  118.4 24.7 %copy-start.36 = (bf16[1024,768]{1,0:T(8,128)(2,1)}, bf16[1024,768]{1,0:T(8,128)(2,1)S(1)}, u32[]{:S(2)}) copy-start(bf16[1024,768]{1,0:T(8,128)(2,1)S(1)} %get-tuple-element.66.attended_ref) | copy-start | bytes 4718596
  145.1 23.3 %copy-start.4 = (f32[1024,768]{1,0:T(8,128)}, f32[1024,768]{1,0:T(8,128)S(1)}, u32[]{:S(2)}) copy-start(f32[1024,768]{1,0:T(8,128)S(1)} %get-tuple-element.71.middle_ref) | copy-start | bytes 9437188
  168.3 24.9 %all-to-all-start = ((bf16[4,256,768]{2,1,0:T(8,128)(2,1)}), bf16[4,256,768]{2,1,0:T(8,128)(2,1)}, u32[]{:S(2)}, u32[]{:S(2)}) async-start(bf16[4,256,768]{2,1,0:T(8,128)(2,1)} %bitcast.54), calls=%async_computation | async-start | bytes 3145728 | tf_op jit(solution)/shard_map/all_to_all | solution.py:651
  266.1 24.5 %all-to-all-start.2 = ((bf16[4,256,768]{2,1,0:T(8,128)(2,1)}), bf16[4,256,768]{2,1,0:T(8,128)(2,1)}, u32[]{:S(2)}, u32[]{:S(2)}) async-start(bf16[4,256,768]{2,1,0:T(8,128)(2,1)} %bitcast.55), calls=%async_computation.2 | async-start | bytes 3145728 | tf_op jit(solution)/shard_map/all_to_all | solution.py:651
  290.6 25.6 %all-to-all-start.3 = ((bf16[4,256,768]{2,1,0:T(8,128)(2,1)}), bf16[4,256,768]{2,1,0:T(8,128)(2,1)}, u32[]{:S(2)}, u32[]{:S(2)}) async-start(bf16[4,256,768]{2,1,0:T(8,128)(2,1)} %bitcast.59), calls=%async_computation.3 | async-start | bytes 3145728 | tf_op jit(solution)/shard_map/all_to_all | solution.py:651
  295.0 166.8 %all-reduce.3.cloned.1.call-start = ((), (), s32[]{:S(2)}) async-start(), calls=%async_computation.15 | async-start | bytes 2752512
  331.9 237.9 %reduce-scatter.5.cloned.1.call-start = ((), (), s32[]{:S(2)}) async-start(), calls=%async_computation.12 | async-start | bytes 3649536 | tf_op jit(solution)/shard_map/reduce_scatter | solution.py:795
  332.8 45.2 %copy-start.39 = (bf16[1024,768]{1,0:T(8,128)(2,1)S(1)}, bf16[1024,768]{1,0:T(8,128)(2,1)}, u32[]{:S(2)}) copy-start(bf16[1024,768]{1,0:T(8,128)(2,1)} %copy-done.38) | copy-start | bytes 4718596
  385.7 261.2 %reduce-scatter.9.cloned.1.call-start = ((), (), s32[]{:S(2)}) async-start(), calls=%async_computation.14 | async-start | bytes 3538944 | tf_op jit(solution)/shard_map/reduce_scatter | solution.py:761
  394.5 373.0 %reduce-scatter.7.cloned.1.call-start = ((), (), s32[]{:S(2)}) async-start(), calls=%async_computation.13 | async-start | bytes 7077888 | tf_op jit(solution)/shard_map/reduce_scatter | solution.py:762
  414.7 12.0 %copy-start.60 = (f32[24,8]{0,1:T(8,128)S(1)}, f32[24,8]{0,1:T(8,128)}, u32[]{:S(2)}) copy-start(f32[24,8]{0,1:T(8,128)} %param.43) | copy-start | bytes 2308
  414.7 12.7 %copy-start.61 = (f32[24,8]{0,1:T(8,128)S(1)}, f32[24,8]{0,1:T(8,128)}, u32[]{:S(2)}) copy-start(f32[24,8]{0,1:T(8,128)} %param.44) | copy-start | bytes 2308
  414.7 13.4 %copy-start.62 = (f32[24,6]{0,1:T(8,128)S(1)}, f32[24,6]{0,1:T(8,128)}, u32[]{:S(2)}) copy-start(f32[24,6]{0,1:T(8,128)} %param.49) | copy-start | bytes 1732
  414.8 14.1 %copy-start.63 = (f32[24,6]{0,1:T(8,128)S(1)}, f32[24,6]{0,1:T(8,128)}, u32[]{:S(2)}) copy-start(f32[24,6]{0,1:T(8,128)} %param.50) | copy-start | bytes 1732
  422.2 10.3 %all-to-all-start.4 = ((f32[32,1,112]{2,1,0:T(1,128)}), f32[32,1,112]{2,1,0:T(1,128)S(1)}, u32[]{:S(2)}, u32[]{:S(2)}) async-start(f32[32,1,112]{2,1,0:T(1,128)} %bitcast.24), calls=%async_computation.5 | async-start | bytes 32768 | tf_op jit(solution)/shard_map/all_to_all | solution.py:651
  648.7 149.5 %copy-start.46 = (f32[1,256,768]{2,1,0:T(8,128)}, f32[1,256,768]{2,1,0:T(8,128)S(1)}, u32[]{:S(2)}) copy-start(f32[1,256,768]{2,1,0:T(8,128)S(1)} %get-tuple-element.380) | copy-start | bytes 2359300
  648.7 145.7 %copy-start.54 = (f32[24,768]{1,0:T(8,128)S(1)}, f32[24,768]{1,0:T(8,128)}, u32[]{:S(2)}) copy-start(f32[24,768]{1,0:T(8,128)} %param.39) | copy-start | bytes 221188
  648.7 147.4 %copy-start.51 = (f32[24,2304]{1,0:T(8,128)S(1)}, f32[24,2304]{1,0:T(8,128)}, u32[]{:S(2)}) copy-start(f32[24,2304]{1,0:T(8,128)} %param.36) | copy-start | bytes 663556
  769.7 30.6 %copy-start.42 = (f32[1,96,4096]{2,1,0:T(8,128)}, f32[1,96,4096]{2,1,0:T(8,128)S(1)}, u32[]{:S(2)}) copy-start(f32[1,96,4096]{2,1,0:T(8,128)S(1)} %get-tuple-element.382) | copy-start | bytes 4718596
  769.7 28.5 %copy-start.45 = (f32[1,256,768]{2,1,0:T(8,128)S(1)}, f32[1,256,768]{2,1,0:T(8,128)}, u32[]{:S(2)}) copy-start(f32[1,256,768]{2,1,0:T(8,128)} %param.57) | copy-start | bytes 2359300
  771.8 10.8 %all-to-all-start.5 = ((f32[32,1,128]{2,1,0:T(1,128)}), f32[32,1,128]{2,1,0:T(1,128)S(1)}, u32[]{:S(2)}, u32[]{:S(2)}) async-start(f32[32,1,128]{2,1,0:T(1,128)} %broadcast_in_dim.45), calls=%async_computation.8 | async-start | bytes 32768 | tf_op jit(solution)/shard_map/all_to_all | solution.py:651
  (47 other events, 131.1 us)
Sparse Core Ops, SparseCore 0:
  12.5 67.0 all-gather.3
  82.4 59.2 all-gather.7
  144.4 97.6 all-gather.5
  332.0 129.7 all-reduce.2
  467.0 102.7 reduce-scatter.4
  573.3 73.5 reduce-scatter.8
  650.4 117.0 reduce-scatter.6
